TPU v7x, 256 devices: a whole 4x4x8 slice. The times are simulated.
256 devices in a mesh: blk: 16 (over z_lo, y, core), ulysses: 16 (over z_hi, x).
Axes of the slice: x: 4, y: 4, z: 8 (z_hi: 4, z_lo: 2; z = z_hi * 2 + z_lo), core: 2. Of those that a mesh axis runs over, the one named last changes fastest.
Arguments:
- query_tokens: bfloat16 [32768, 4096], P(('blk', 'ulysses')), may hold values from -5 to 5
- key_tokens: bfloat16 [32768, 4096], P(('blk', 'ulysses')), may hold values from -5 to 5
- value_tokens: bfloat16 [32768, 4096], P(('blk', 'ulysses')), may hold values from -5 to 5
- cotangent: bfloat16 [32768, 4096], P(('blk', 'ulysses')), may hold values from -5 to 5
- block_mask: int32 [256, 256], replicated, may hold values from 0 to 1, as said below
Outputs:
- attended: bfloat16 [32768, 4096], P(('blk', 'ulysses'))
- grad_query: bfloat16 [32768, 4096], P(('blk', 'ulysses'))
- grad_key: bfloat16 [32768, 4096], P(('blk', 'ulysses'))
- grad_value: bfloat16 [32768, 4096], P(('blk', 'ulysses'))
Inputs may be any that keep to these rules, and one draw needn't show every extreme that they name: block_mask is symmetric. A span is a run of 16 consecutive blocks. Inside a span, block s attends block s2 exactly when they differ by at most one. A query block attends at most one key block in each other span. The queries of one span attend keys of exactly 7 other spans, and at most 2 distinct key blocks of any other span; in every draw some pairs of spans reach 2.
All inputs are finite; a program needn't handle non-finite values.
Results may differ from a plain program's by a relative error of at most 0.0096.
Values may be sent and summed in bfloat16 or wider, within the bound.
A program may use at most 128 MiB of HBM per device.

v0:
```python
import jax
import jax.numpy as jnp
from jax import lax
from jax.sharding import PartitionSpec as P

HEAD_DIM = 128
BLOCK = 128
NEED = 2


def lists_from(flag_rows, list_width):
    columns = flag_rows.shape[-1]
    ranking = flag_rows * columns + (
        columns - 1 - lax.broadcasted_iota(jnp.int32, flag_rows.shape, flag_rows.ndim - 1)
    )
    values_top, indices = lax.top_k(ranking, list_width)
    return (indices, values_top >= columns)


def segment_add(selector, tensor, form):
    return jnp.einsum(form, selector, tensor, precision=lax.Precision.HIGHEST)


def shards(query_tokens, key_tokens, value_tokens, cotangent, block_mask):
    groups = lax.axis_size("blk")
    group_id = lax.axis_index("blk")
    heads_q, heads_k, heads_v, heads_g = (
        lax.all_to_all(query_tokens, "ulysses", split_axis=1, concat_axis=0, tiled=True),
        lax.all_to_all(key_tokens, "ulysses", split_axis=1, concat_axis=0, tiled=True),
        lax.all_to_all(value_tokens, "ulysses", split_axis=1, concat_axis=0, tiled=True),
        lax.all_to_all(cotangent, "ulysses", split_axis=1, concat_axis=0, tiled=True),
    )
    span_len = heads_q.shape[0] // BLOCK
    local_heads = heads_q.shape[1] // HEAD_DIM
    score_scale = HEAD_DIM ** (-0.5)

    def blocked(tensor):
        return tensor.reshape(span_len, BLOCK, local_heads, HEAD_DIM)

    def tokens_of(tensor):
        return tensor.reshape(span_len * BLOCK, local_heads * HEAD_DIM).astype(jnp.bfloat16)

    q_blocks = blocked(heads_q)
    k_blocks = blocked(heads_k)
    v_blocks = blocked(heads_v)
    g_blocks = blocked(heads_g)
    first_row = group_id * span_len
    my_rows = lax.dynamic_slice_in_dim(block_mask, first_row, span_len, 0)
    my_cols = lax.dynamic_slice_in_dim(block_mask, first_row, span_len, 1)
    own_flags = lax.dynamic_slice_in_dim(my_rows, first_row, span_len, 1)
    own_index, own_valid = lists_from(own_flags, 3)
    others = (lax.broadcasted_iota(jnp.int32, (groups, 1), 0) != group_id).astype(jnp.int32)
    row_cube = my_rows.reshape(span_len, groups, span_len)
    fetch_index, fetch_valid = lists_from(jnp.max(row_cube, axis=0) * others, NEED)
    col_cube = my_cols.reshape(groups, span_len, span_len)
    send_index, send_valid = lists_from(jnp.max(col_cube, axis=1) * others, NEED)
    sent_k = k_blocks[send_index]
    sent_v = v_blocks[send_index]
    fetched_k, fetched_v = (
        lax.all_to_all(sent_k, "blk", split_axis=0, concat_axis=0, tiled=True),
        lax.all_to_all(sent_v, "blk", split_axis=0, concat_axis=0, tiled=True),
    )
    spot_iota = lax.broadcasted_iota(jnp.int32, (groups, NEED, span_len), 2)
    fetch_pick = (fetch_index[:, :, None] == spot_iota).astype(jnp.int32)
    attach = jnp.sum(row_cube.transpose(1, 0, 2)[:, None, :, :] * fetch_pick[:, :, None, :], axis=3)
    attach = attach * fetch_valid[:, :, None].astype(jnp.int32)
    query_pick = jnp.sum(attach * spot_iota, axis=2)
    attach_f = attach.astype(jnp.float32)
    own_k = k_blocks[own_index]
    own_v = v_blocks[own_index]
    own_scores = (
        jnp.einsum("irhd,itchd->ithrc", q_blocks, own_k, preferred_element_type=jnp.float32)
        * score_scale
    )
    own_scores = jnp.where(own_valid[:, :, None, None, None], own_scores, -jnp.inf)
    cross_q = q_blocks[query_pick]
    cross_g = g_blocks[query_pick]
    cross_scores = (
        jnp.einsum("curhd,cukhd->cuhrk", cross_q, fetched_k, preferred_element_type=jnp.float32)
        * score_scale
    )
    cross_scores = jnp.where(fetch_valid[:, :, None, None, None], cross_scores, -jnp.inf)
    tile_peak = jnp.max(cross_scores, axis=4)
    cross_peak = jnp.max(
        jnp.where(attach[:, :, :, None, None] > 0, tile_peak[:, :, None], -jnp.inf), axis=(0, 1)
    )
    row_peak = jnp.maximum(jnp.max(own_scores, axis=(1, 4)), cross_peak)
    own_total = jnp.sum(jnp.exp(own_scores - row_peak[:, None, :, :, None]), axis=(1, 4))
    cross_sums = jnp.sum(jnp.exp(cross_scores - row_peak[query_pick][..., None]), axis=4)
    row_total = own_total + segment_add(attach_f, cross_sums, "cui,cuhr->ihr")
    log_total = row_peak + jnp.log(row_total)
    cross_log = log_total[query_pick]
    own_prob = jnp.exp(own_scores - log_total[:, None, :, :, None])
    cross_prob = jnp.exp(cross_scores - cross_log[..., None])
    own_weights = own_prob.astype(jnp.bfloat16)
    cross_weights = cross_prob.astype(jnp.bfloat16)
    cross_out = jnp.einsum(
        "cuhrk,cukhd->curhd", cross_weights, fetched_v, preferred_element_type=jnp.float32
    )
    output = jnp.einsum("ithrc,itchd->irhd", own_weights, own_v, preferred_element_type=jnp.float32)
    output = output + segment_add(attach_f, cross_out, "cui,curhd->irhd")
    row_delta = jnp.sum(g_blocks.astype(jnp.float32) * output, axis=3).transpose(0, 2, 1)
    cross_delta = row_delta[query_pick]
    own_dprob = jnp.einsum("irhd,itchd->ithrc", g_blocks, own_v, preferred_element_type=jnp.float32)
    own_dscore = (own_prob * (own_dprob - row_delta[:, None, :, :, None])).astype(jnp.bfloat16)
    grad_q = score_scale * jnp.einsum(
        "ithrc,itchd->irhd", own_dscore, own_k, preferred_element_type=jnp.float32
    )
    own_dk = score_scale * jnp.einsum(
        "ithrc,irhd->itchd", own_dscore, q_blocks, preferred_element_type=jnp.float32
    )
    own_dv = jnp.einsum(
        "ithrc,irhd->itchd", own_weights, g_blocks, preferred_element_type=jnp.float32
    )
    empty_grad = jnp.zeros((span_len, BLOCK, local_heads, HEAD_DIM), jnp.float32)
    grad_k = empty_grad.at[own_index].add(own_dk)
    grad_v = empty_grad.at[own_index].add(own_dv)
    cross_dprob = jnp.einsum(
        "curhd,cukhd->cuhrk", cross_g, fetched_v, preferred_element_type=jnp.float32
    )
    cross_dscore = (cross_prob * (cross_dprob - cross_delta[..., None])).astype(jnp.bfloat16)
    cross_dq = score_scale * jnp.einsum(
        "cuhrk,cukhd->curhd", cross_dscore, fetched_k, preferred_element_type=jnp.float32
    )
    grad_q = grad_q + segment_add(attach_f, cross_dq, "cui,curhd->irhd")
    part_k = score_scale * jnp.einsum(
        "cuhrk,curhd->cukhd", cross_dscore, cross_q, preferred_element_type=jnp.float32
    )
    part_v = jnp.einsum(
        "cuhrk,curhd->cukhd", cross_weights, cross_g, preferred_element_type=jnp.float32
    )
    back_k, back_v = (
        lax.all_to_all(part_k, "blk", split_axis=0, concat_axis=0, tiled=True),
        lax.all_to_all(part_v, "blk", split_axis=0, concat_axis=0, tiled=True),
    )
    send_pick = ((send_index[:, :, None] == spot_iota) & send_valid[:, :, None]).astype(jnp.float32)
    grad_k = grad_k + segment_add(send_pick, back_k, "buj,bukhd->jkhd")
    grad_v = grad_v + segment_add(send_pick, back_v, "buj,bukhd->jkhd")
    attended, grad_query, grad_key, grad_value = (
        lax.all_to_all(tokens_of(output), "ulysses", split_axis=0, concat_axis=1, tiled=True),
        lax.all_to_all(tokens_of(grad_q), "ulysses", split_axis=0, concat_axis=1, tiled=True),
        lax.all_to_all(tokens_of(grad_k), "ulysses", split_axis=0, concat_axis=1, tiled=True),
        lax.all_to_all(tokens_of(grad_v), "ulysses", split_axis=0, concat_axis=1, tiled=True),
    )
    return (attended, grad_query, grad_key, grad_value)


def solution(mesh):
    placed = (
        P(("blk", "ulysses"), None),
        P(("blk", "ulysses"), None),
        P(("blk", "ulysses"), None),
        P(("blk", "ulysses"), None),
        P(),
    )
    return jax.shard_map(
        shards,
        mesh=mesh,
        in_specs=placed,
        out_specs=(
            P(("blk", "ulysses"), None),
            P(("blk", "ulysses"), None),
            P(("blk", "ulysses"), None),
            P(("blk", "ulysses"), None),
        ),
        check_vma=False,
    )
```

profile of v0, /device:TPU:56, one launch (start us, length us, event | category | flops | bytes accessed | tf_op | source)
XLA Modules:
  0.0 528.4 jit_solution(7634061339372673453)
XLA Ops:
  3.1 10.1 %all-to-all-start.6 = ((bf16[128,16,256]{0,2,1:T(8,128)(2,1)}), bf16[128,16,256]{0,2,1:T(8,128)(2,1)S(1)}, u32[]{:S(2)}, u32[]{:S(2)}) async-start(bf16[128,16,256]{0,2,1:T(8,128)(2,1)} %bitcast.41), calls=%async_computation.6 | async-start | bytes 2097152 | tf_op jit(solution)/shard_map/all_to_all | solution.py:31
  14.5 27.8 %all-to-all-done.6 = bf16[128,16,256]{0,2,1:T(8,128)(2,1)S(1)} async-done(((bf16[128,16,256]{0,2,1:T(8,128)(2,1)}), bf16[128,16,256]{0,2,1:T(8,128)(2,1)S(1)}, u32[]{:S(2)}, u32[]{:S(2)}) %all-to-all-start.6) | async-done | bytes 1048608 | tf_op jit(solution)/shard_map/all_to_all | solution.py:31
  47.8 20.7 %all-to-all-done = bf16[128,16,256]{0,2,1:T(8,128)(2,1)S(1)} async-done(((bf16[128,16,256]{0,2,1:T(8,128)(2,1)}), bf16[128,16,256]{0,2,1:T(8,128)(2,1)S(1)}, u32[]{:S(2)}, u32[]{:S(2)}) %all-to-all-start) | async-done | bytes 1048608 | tf_op jit(solution)/shard_map/all_to_all | solution.py:30
  68.5 10.5 %all-to-all-start.1 = ((bf16[128,16,256]{0,2,1:T(8,128)(2,1)}), bf16[128,16,256]{0,2,1:T(8,128)(2,1)S(1)}, u32[]{:S(2)}, u32[]{:S(2)}) async-start(bf16[128,16,256]{0,2,1:T(8,128)(2,1)} %bitcast.197), calls=%async_computation.1 | async-start | bytes 2097152 | tf_op jit(solution)/shard_map/all_to_all | solution.py:29
  81.3 18.1 %all-to-all-done.1 = bf16[128,16,256]{0,2,1:T(8,128)(2,1)S(1)} async-done(((bf16[128,16,256]{0,2,1:T(8,128)(2,1)}), bf16[128,16,256]{0,2,1:T(8,128)(2,1)S(1)}, u32[]{:S(2)}, u32[]{:S(2)}) %all-to-all-start.1) | async-done | bytes 1048608 | tf_op jit(solution)/shard_map/all_to_all | solution.py:29
  99.3 10.3 %all-to-all-start.2 = ((bf16[128,16,256]{0,2,1:T(8,128)(2,1)}), bf16[128,16,256]{0,2,1:T(8,128)(2,1)S(1)}, u32[]{:S(2)}, u32[]{:S(2)}) async-start(bf16[128,16,256]{0,2,1:T(8,128)(2,1)} %bitcast.195), calls=%async_computation.2 | async-start | bytes 2097152 | tf_op jit(solution)/shard_map/all_to_all | solution.py:28
  115.1 21.1 %all-to-all-done.2 = bf16[128,16,256]{0,2,1:T(8,128)(2,1)S(1)} async-done(((bf16[128,16,256]{0,2,1:T(8,128)(2,1)}), bf16[128,16,256]{0,2,1:T(8,128)(2,1)S(1)}, u32[]{:S(2)}, u32[]{:S(2)}) %all-to-all-start.2) | async-done | bytes 1048608 | tf_op jit(solution)/shard_map/all_to_all | solution.py:28
  151.1 19.7 %all-to-all-done.3 = bf16[16,2,128,2,128]{4,2,3,1,0:T(8,128)(2,1)} async-done(((bf16[16,2,128,2,128]{4,2,3,1,0:T(8,128)(2,1)}), bf16[16,2,128,2,128]{4,2,3,1,0:T(8,128)(2,1)}, u32[]{:S(2)}, u32[]{:S(2)}) %all-to-all-start.3) | async-done | bytes 2097184 | tf_op jit(solution)/shard_map/all_to_all | solution.py:60
  170.8 5.8 %all-to-all-start.4 = ((bf16[16,2,128,2,128]{2,4,3,1,0:T(8,128)(2,1)}), bf16[16,2,128,2,128]{2,4,3,1,0:T(8,128)(2,1)}, u32[]{:S(2)}, u32[]{:S(2)}) async-start(bf16[16,2,128,2,128]{2,4,3,1,0:T(8,128)(2,1)} %bitcast.190), calls=%async_computation.4 | async-start | bytes 4194304 | tf_op jit(solution)/shard_map/all_to_all | solution.py:61
  217.6 6.2 %convolution_bitcast_fusion.2 = f32[16,2,128,2,128]{2,4,3,1,0:T(8,128)} fusion(bf16[16,2,128,2,128]{2,4,3,1,0:T(8,128)(2,1)} %all-to-all-done.4, f32[16,2,2,128,128]{3,4,2,1,0:T(8,128)} %get-tuple-element.58, f32[16,2,2,128]{3,2,1,0:T(2,128)S(1)} %bitcast.198, pred[16,2]{1,0:T(8,128)(4,1)S(1)} %copy.351), kind=kOutput, calls=%fused_computation.36 | convolution fusion | flops 272629760 | bytes 10518560 | tf_op jit(solution)/shard_map/cuhrk,cukhd->curhd/dot_general | solution.py:97
  237.2 7.9 %multiply_reduce_fusion = (f32[16,128,2]{1,2,0:T(2,128)S(1)}, bf16[16,128,2,128]{1,3,2,0:T(8,128)(2,1)}) fusion(bf16[128,16,256]{0,2,1:T(8,128)(2,1)} %copy-done, f32[16,128,2,128]{1,3,2,0:T(8,128)} %copy.374, bf16[16,3,128,2,128]{4,2,1,3,0:T(8,128)(2,1)} %copy.410, f32[16,2,3,128,128]{4,3,2,1,0:T(8,128)} %get-tuple-element.60, ...), kind=kOutput, calls=%fused_computation.41 | convolution fusion | flops 411561984 | bytes 13664304 | tf_op jit(solution)/shard_map/ithrc,itchd->irhd/dot_general | solution.py:100
  259.2 5.8 %fusion.12 = f32[16,128,2,128]{3,0,2,1:T(8,128)} fusion(f32[16,2,128,2,128]{4,2,3,1,0:T(8,128)S(1)} %multiply_bitcast_fusion.2, s32[16,2,16]{2,1,0:T(2,128)S(1)} %multiply_reduce_fusion.1, s32[16,2]{0,1:T(2,128)S(1)} %get-tuple-element.46), kind=kOutput, calls=%fused_computation.42 | convolution fusion | flops 201327616 | bytes 6293632 | tf_op jit(solution)/shard_map/cui,curhd->irhd/dot_general | solution.py:21
  268.0 6.0 %fusion = bf16[16,3,2,128,128]{3,4,1,2,0:T(8,128)(2,1)S(1)} fusion(f32[16,2,3,128,128]{4,3,2,1,0:T(8,128)} %get-tuple-element.60, f32[16,2,128]{2,1,0:T(2,128)S(1)} %bitcast.203, f32[16,2,128]{2,1,0:T(2,128)S(1)} %copy.365, pred[16,3]{1,0:T(8,128)(4,1)S(1)} %copy.340, bf16[16,3,128,2,128]{4,2,1,3,0:T(8,128)(2,1)} %copy.410, ...), kind=kOutput, calls=%fused_computation.12 | convolution fusion | flops 412090368 | bytes 13664304 | tf_op jit(solution)/shard_map/irhd,itchd->ithrc/dot_general | solution.py:104
  281.2 6.5 %all-to-all-start.7 = ((bf16[16,128,256]{1,2,0:T(8,128)(2,1)}), bf16[16,128,256]{1,2,0:T(8,128)(2,1)S(1)}, u32[]{:S(2)}, u32[]{:S(2)}) async-start(bf16[16,128,256]{1,2,0:T(8,128)(2,1)} %bitcast.193), calls=%async_computation.7 | async-start | bytes 2097152 | tf_op jit(solution)/shard_map/all_to_all | solution.py:141
  287.8 5.8 %multiply_bitcast_fusion.1 = f32[16,2,128,2,128]{4,2,3,1,0:T(8,128)} fusion(bf16[16,2,128,2,128]{2,4,3,1,0:T(8,128)(2,1)} %bitcast.184, bf16[16,2,2,128,128]{3,4,2,1,0:T(8,128)(2,1)} %copy-done.6), kind=kOutput, calls=%fused_computation.26 | convolution fusion | flops 269484032 | bytes 8388608 | tf_op jit(solution)/shard_map/cuhrk,curhd->cukhd/dot_general | solution.py:126
  293.5 24.9 %all-to-all-done.7 = bf16[16,128,256]{1,2,0:T(8,128)(2,1)S(1)} async-done(((bf16[16,128,256]{1,2,0:T(8,128)(2,1)}), bf16[16,128,256]{1,2,0:T(8,128)(2,1)S(1)}, u32[]{:S(2)}, u32[]{:S(2)}) %all-to-all-start.7) | async-done | bytes 1048608 | tf_op jit(solution)/shard_map/all_to_all | solution.py:141
  324.1 5.8 %convolution_bitcast_fusion.1 = f32[16,2,128,2,128]{2,4,3,1,0:T(8,128)} fusion(bf16[16,2,128,2,128]{2,4,3,1,0:T(8,128)(2,1)S(1)} %bitcast.187, f32[16,2,2,128,128]{3,4,2,1,0:T(8,128)} %get-tuple-element.58, f32[16,2,2,128]{3,2,1,0:T(2,128)S(1)} %bitcast.200, pred[16,2]{1,0:T(8,128)(4,1)S(1)} %copy.351), kind=kOutput, calls=%fused_computation.35 | convolution fusion | flops 272629760 | bytes 10518560 | tf_op jit(solution)/shard_map/cuhrk,curhd->cukhd/dot_general | solution.py:129
  329.9 55.9 %all-to-all-done.8 = f32[16,2,128,2,128]{4,2,3,1,0:T(8,128)} async-done(((f32[16,2,128,2,128]{4,2,3,1,0:T(8,128)}), f32[16,2,128,2,128]{4,2,3,1,0:T(8,128)}, u32[]{:S(2)}, u32[]{:S(2)}) %all-to-all-start.8) | async-done | bytes 4194336 | tf_op jit(solution)/shard_map/all_to_all | solution.py:133
  397.3 5.9 %fusion.15 = f32[16,128,2,128]{3,0,2,1:T(8,128)S(1)} fusion(f32[16,2,128,2,128]{4,2,3,1,0:T(8,128)} %all-to-all-done.8, s32[16,2]{0,1:T(2,128)S(1)} %get-tuple-element.52, pred[16,2]{0,1:T(4,128)(4,1)S(1)} %slice_compare_fusion.1), kind=kOutput, calls=%fused_computation.43 | convolution fusion | flops 201327616 | bytes 6291616 | tf_op jit(solution)/shard_map/buj,bukhd->jkhd/dot_general | solution.py:21
  404.4 9.4 %scatter_fusion = f32[16,128,2,128]{3,1,2,0:T(8,128)S(1)} fusion(f32[16,128,2,128]{3,1,2,0:T(8,128)S(1)} %copy.396, s32[48]{0:T(128)S(1)} %reshape.124, f32[48,128,2,128]{3,1,2,0:T(8,128)} %bitcast.183), kind=kCustom, calls=%fused_computation.9 | custom fusion | flops 1572864 | bytes 18874560 | tf_op jit(solution)/shard_map/scatter-add | solution.py:116
  417.2 35.7 %all-to-all-done.10 = f32[16,2,128,2,128]{2,4,3,1,0:T(8,128)} async-done(((f32[16,2,128,2,128]{2,4,3,1,0:T(8,128)}), f32[16,2,128,2,128]{2,4,3,1,0:T(8,128)}, u32[]{:S(2)}, u32[]{:S(2)}) %all-to-all-start.10) | async-done | bytes 4194336 | tf_op jit(solution)/shard_map/all_to_all | solution.py:134
  475.6 9.4 %scatter_fusion.1 = f32[16,128,2,128]{3,1,2,0:T(8,128)S(1)} fusion(f32[16,128,2,128]{3,1,2,0:T(8,128)S(1)} %copy.402, s32[48]{0:T(128)S(1)} %reshape.124, f32[48,128,2,128]{3,1,2,0:T(8,128)} %bitcast.182), kind=kCustom, calls=%fused_computation.10 | custom fusion | flops 1572864 | bytes 18874560 | tf_op jit(solution)/shard_map/scatter-add | solution.py:117
  488.9 7.3 %all-to-all-start.11 = ((bf16[16,128,256]{1,2,0:T(8,128)(2,1)}), bf16[16,128,256]{1,2,0:T(8,128)(2,1)S(1)}, u32[]{:S(2)}, u32[]{:S(2)}) async-start(bf16[16,128,256]{1,2,0:T(8,128)(2,1)} %bitcast.78), calls=%async_computation.11 | async-start | bytes 2097152 | tf_op jit(solution)/shard_map/all_to_all | solution.py:143
  502.0 24.8 %all-to-all-done.11 = bf16[16,128,256]{1,2,0:T(8,128)(2,1)S(1)} async-done(((bf16[16,128,256]{1,2,0:T(8,128)(2,1)}), bf16[16,128,256]{1,2,0:T(8,128)(2,1)S(1)}, u32[]{:S(2)}, u32[]{:S(2)}) %all-to-all-start.11) | async-done | bytes 1048608 | tf_op jit(solution)/shard_map/all_to_all | solution.py:143
  (128 shorter events, 165.7 us)
Async XLA Ops:
  0.6 12.6 %copy-start.11 = (bf16[128,4096]{1,0:T(8,128)(2,1)S(1)}, bf16[128,4096]{1,0:T(8,128)(2,1)}, u32[]{:S(2)}) copy-start(bf16[128,4096]{1,0:T(8,128)(2,1)} %param.7) | copy-start | bytes 3145732
  0.6 45.8 %copy-start.12 = (bf16[128,4096]{1,0:T(8,128)(2,1)S(1)}, bf16[128,4096]{1,0:T(8,128)(2,1)}, u32[]{:S(2)}) copy-start(bf16[128,4096]{1,0:T(8,128)(2,1)} %param.6) | copy-start | bytes 3145732
  3.1 39.3 %all-to-all-start.6 = ((bf16[128,16,256]{0,2,1:T(8,128)(2,1)}), bf16[128,16,256]{0,2,1:T(8,128)(2,1)S(1)}, u32[]{:S(2)}, u32[]{:S(2)}) async-start(bf16[128,16,256]{0,2,1:T(8,128)(2,1)} %bitcast.41), calls=%async_computation.6 | async-start | bytes 2097152 | tf_op jit(solution)/shard_map/all_to_all | solution.py:31
  42.3 38.9 %copy-start = (bf16[128,16,256]{0,2,1:T(8,128)(2,1)}, bf16[128,16,256]{0,2,1:T(8,128)(2,1)S(1)}, u32[]{:S(2)}) copy-start(bf16[128,16,256]{0,2,1:T(8,128)(2,1)S(1)} %all-to-all-done.6) | copy-start | bytes 3145732
  42.3 26.2 %all-to-all-start = ((bf16[128,16,256]{0,2,1:T(8,128)(2,1)}), bf16[128,16,256]{0,2,1:T(8,128)(2,1)S(1)}, u32[]{:S(2)}, u32[]{:S(2)}) async-start(bf16[128,16,256]{0,2,1:T(8,128)(2,1)} %bitcast), calls=%async_computation | async-start | bytes 2097152 | tf_op jit(solution)/shard_map/all_to_all | solution.py:30
  46.4 63.2 %copy-start.13 = (s32[256,256]{1,0:T(8,128)S(1)}, s32[256,256]{1,0:T(8,128)}, u32[]{:S(2)}) copy-start(s32[256,256]{1,0:T(8,128)} %param.9) | copy-start | bytes 786436
  68.5 30.9 %all-to-all-start.1 = ((bf16[128,16,256]{0,2,1:T(8,128)(2,1)}), bf16[128,16,256]{0,2,1:T(8,128)(2,1)S(1)}, u32[]{:S(2)}, u32[]{:S(2)}) async-start(bf16[128,16,256]{0,2,1:T(8,128)(2,1)} %bitcast.197), calls=%async_computation.1 | async-start | bytes 2097152 | tf_op jit(solution)/shard_map/all_to_all | solution.py:29
  99.3 36.9 %all-to-all-start.2 = ((bf16[128,16,256]{0,2,1:T(8,128)(2,1)}), bf16[128,16,256]{0,2,1:T(8,128)(2,1)S(1)}, u32[]{:S(2)}, u32[]{:S(2)}) async-start(bf16[128,16,256]{0,2,1:T(8,128)(2,1)} %bitcast.195), calls=%async_computation.2 | async-start | bytes 2097152 | tf_op jit(solution)/shard_map/all_to_all | solution.py:28
  136.2 10.8 %copy-start.2 = (bf16[128,16,256]{0,2,1:T(8,128)(2,1)}, bf16[128,16,256]{0,2,1:T(8,128)(2,1)S(1)}, u32[]{:S(2)}) copy-start(bf16[128,16,256]{0,2,1:T(8,128)(2,1)S(1)} %all-to-all-done.2) | copy-start | bytes 3145732
  136.2 34.6 %all-to-all-start.3 = ((bf16[16,2,128,2,128]{4,2,3,1,0:T(8,128)(2,1)}), bf16[16,2,128,2,128]{4,2,3,1,0:T(8,128)(2,1)}, u32[]{:S(2)}, u32[]{:S(2)}) async-start(bf16[16,2,128,2,128]{4,2,3,1,0:T(8,128)(2,1)} %bitcast.191), calls=%async_computation.3 | async-start | bytes 4194304 | tf_op jit(solution)/shard_map/all_to_all | solution.py:60
  170.8 46.8 %all-to-all-start.4 = ((bf16[16,2,128,2,128]{2,4,3,1,0:T(8,128)(2,1)}), bf16[16,2,128,2,128]{2,4,3,1,0:T(8,128)(2,1)}, u32[]{:S(2)}, u32[]{:S(2)}) async-start(bf16[16,2,128,2,128]{2,4,3,1,0:T(8,128)(2,1)} %bitcast.190), calls=%async_computation.4 | async-start | bytes 4194304 | tf_op jit(solution)/shard_map/all_to_all | solution.py:61
  198.6 5.0 copy-start.4
  245.2 36.1 %all-to-all-start.5 = ((bf16[16,128,256]{1,2,0:T(8,128)(2,1)}), bf16[16,128,256]{1,2,0:T(8,128)(2,1)}, u32[]{:S(2)}, u32[]{:S(2)}) async-start(bf16[16,128,256]{1,2,0:T(8,128)(2,1)} %bitcast.192), calls=%async_computation.5 | async-start | bytes 2097152 | tf_op jit(solution)/shard_map/all_to_all | solution.py:140
  268.0 7.6 %copy-start.8 = (f32[16,128,2,128]{1,3,2,0:T(8,128)S(1)}, f32[16,128,2,128]{1,3,2,0:T(8,128)}, u32[]{:S(2)}) copy-start(f32[16,128,2,128]{1,3,2,0:T(8,128)} %copy.389) | copy-start | bytes 6291460
  281.2 37.2 %all-to-all-start.7 = ((bf16[16,128,256]{1,2,0:T(8,128)(2,1)}), bf16[16,128,256]{1,2,0:T(8,128)(2,1)S(1)}, u32[]{:S(2)}, u32[]{:S(2)}) async-start(bf16[16,128,256]{1,2,0:T(8,128)(2,1)} %bitcast.193), calls=%async_computation.7 | async-start | bytes 2097152 | tf_op jit(solution)/shard_map/all_to_all | solution.py:141
  293.5 30.6 %copy-start.5 = (bf16[32,128,2,128]{1,3,2,0:T(8,128)(2,1)S(1)}, bf16[32,128,2,128]{1,3,2,0:T(8,128)(2,1)}, u32[]{:S(2)}) copy-start(bf16[32,128,2,128]{1,3,2,0:T(8,128)(2,1)} %gather_fusion.7) | copy-start | bytes 6291460
  318.4 11.5 %copy-start.9 = (bf16[16,128,256]{1,2,0:T(8,128)(2,1)}, bf16[16,128,256]{1,2,0:T(8,128)(2,1)S(1)}, u32[]{:S(2)}) copy-start(bf16[16,128,256]{1,2,0:T(8,128)(2,1)S(1)} %all-to-all-done.7) | copy-start | bytes 3145732
  318.4 67.4 %all-to-all-start.8 = ((f32[16,2,128,2,128]{4,2,3,1,0:T(8,128)}), f32[16,2,128,2,128]{4,2,3,1,0:T(8,128)}, u32[]{:S(2)}, u32[]{:S(2)}) async-start(f32[16,2,128,2,128]{4,2,3,1,0:T(8,128)} %multiply_bitcast_fusion.1), calls=%async_computation.8 | async-start | bytes 8388608 | tf_op jit(solution)/shard_map/all_to_all | solution.py:133
  329.9 61.3 %copy-start.3 = (bf16[128,16,256]{0,2,1:T(8,128)(2,1)S(1)}, bf16[128,16,256]{0,2,1:T(8,128)(2,1)}, u32[]{:S(2)}) copy-start(bf16[128,16,256]{0,2,1:T(8,128)(2,1)} %copy-done.2) | copy-start | bytes 3145732
  385.8 67.1 %all-to-all-start.10 = ((f32[16,2,128,2,128]{2,4,3,1,0:T(8,128)}), f32[16,2,128,2,128]{2,4,3,1,0:T(8,128)}, u32[]{:S(2)}, u32[]{:S(2)}) async-start(f32[16,2,128,2,128]{2,4,3,1,0:T(8,128)} %convolution_bitcast_fusion.1), calls=%async_computation.10 | async-start | bytes 8388608 | tf_op jit(solution)/shard_map/all_to_all | solution.py:134
  413.8 43.7 %copy-start.1 = (bf16[128,16,256]{0,2,1:T(8,128)(2,1)S(1)}, bf16[128,16,256]{0,2,1:T(8,128)(2,1)}, u32[]{:S(2)}) copy-start(bf16[128,16,256]{0,2,1:T(8,128)(2,1)} %copy-done) | copy-start | bytes 3145732
  452.9 36.0 %all-to-all-start.9 = ((bf16[16,128,256]{1,2,0:T(8,128)(2,1)}), bf16[16,128,256]{1,2,0:T(8,128)(2,1)}, u32[]{:S(2)}, u32[]{:S(2)}) async-start(bf16[16,128,256]{1,2,0:T(8,128)(2,1)} %bitcast.68), calls=%async_computation.9 | async-start | bytes 2097152 | tf_op jit(solution)/shard_map/all_to_all | solution.py:142
  485.2 13.3 %copy-start.10 = (bf16[16,128,256]{1,2,0:T(8,128)(2,1)S(1)}, bf16[16,128,256]{1,2,0:T(8,128)(2,1)}, u32[]{:S(2)}) copy-start(bf16[16,128,256]{1,2,0:T(8,128)(2,1)} %copy-done.9) | copy-start | bytes 3145732
  488.9 37.9 %all-to-all-start.11 = ((bf16[16,128,256]{1,2,0:T(8,128)(2,1)}), bf16[16,128,256]{1,2,0:T(8,128)(2,1)S(1)}, u32[]{:S(2)}, u32[]{:S(2)}) async-start(bf16[16,128,256]{1,2,0:T(8,128)(2,1)} %bitcast.78), calls=%async_computation.11 | async-start | bytes 2097152 | tf_op jit(solution)/shard_map/all_to_all | solution.py:143
  (2 other events, 4.9 us)
where the time goes:
time: 534 us; the launch traced here: 528 us
  waiting for transfers between devices  254 us (48%)
  local copies, waits for them, and re-layouts  82.5 us (15%)
  starting transfers between devices  80.7 us (15%)
  matrix products  79.8 us (15%)
  other arithmetic  29.6 us (6%)
    all_to_all x1, waiting for transfers between devices, shards(): lax.all_to_all(part_k, 'blk', split_axis=0, concat_axis=0, tiled=True)  55.9 us
    all_to_all x1, waiting for transfers between devices, shards(): lax.all_to_all(part_v, 'blk', split_axis=0, concat_axis=0, tiled=True)  35.7 us
    all_to_all x1, waiting for transfers between devices, shards(): lax.all_to_all(cotangent, 'ulysses', split_axis=1, concat_axis=0, tiled=T...  27.8 us
    all_to_all x1, waiting for transfers between devices, shards(): lax.all_to_all(tokens_of(grad_q), 'ulysses', split_axis=0, concat_axis=1,...  24.9 us
    all_to_all x1, waiting for transfers between devices, shards(): lax.all_to_all(tokens_of(grad_v), 'ulysses', split_axis=0, concat_axis=1,...  24.8 us
    all_to_all x1, waiting for transfers between devices, shards(): lax.all_to_all(query_tokens, 'ulysses', split_axis=1, concat_axis=0, tile...  21.1 us
    dot_general x5, matrix products, segment_add(): return jnp.einsum(form, selector, tensor, precision=lax.Precision.HIGHEST)  20.8 us
    all_to_all x1, waiting for transfers between devices, shards(): lax.all_to_all(value_tokens, 'ulysses', split_axis=1, concat_axis=0, tile...  20.7 us
  transfers between devices with their start and end apart: 12, of which 11 were waited for; matrix products, arithmetic and copies ran while one was open for 30% of the time, Pallas kernels for 0%

commit v1 on v0

v1 whole, which is shorter than its diff:
```python
import functools

import jax
import jax.numpy as jnp
from jax import lax
from jax.experimental import pallas as pl
from jax.experimental.pallas import tpu as pltpu
from jax.sharding import PartitionSpec as P

HEAD_DIM = 128
BLOCK = 128
NEED = 2
LINKS = 7
MESH = pl.DeviceIdType.MESH
BF16 = jnp.bfloat16
F32 = jnp.float32
ANY = pl.BlockSpec(memory_space=pl.ANY)
VMEM = pl.BlockSpec(memory_space=pltpu.VMEM)
SMEM = pl.BlockSpec(memory_space=pltpu.SMEM)


def greet(groups, members):
    b, u = lax.axis_index("blk"), lax.axis_index("ulysses")
    barrier = pltpu.get_barrier_semaphore()
    for t in range(1, members):
        pl.semaphore_signal(
            barrier, inc=1, device_id=(b, lax.rem(u + t, members)), device_id_type=MESH
        )
    for t in range(1, groups):
        pl.semaphore_signal(
            barrier, inc=1, device_id=(lax.rem(b + t, groups), u), device_id_type=MESH
        )
    pl.semaphore_wait(barrier, members + groups - 2)


def wait_bytes(ref, sem):
    pltpu.make_async_copy(ref, ref, sem).wait()


def columns(index, width):
    return pl.ds(pl.multiple_of(index * width, width), width)


def gather_kernel(
    groups, members, pick, q, k, v, g, hq, hk, hv, hg, fk, fv,
    land_k, land_v, slots_k, slots_v, send, recv, own, blk_send, blk_recv,
):
    b, u = lax.axis_index("blk"), lax.axis_index("ulysses")
    width = land_k.shape[2]
    greet(groups, members)
    pairs = ((k, land_k), (v, land_v), (q, hq), (g, hg))

    def spread(n):
        src, dst = pairs[n]
        for t in range(1, members):
            to = lax.rem(u + t, members)
            pltpu.make_async_remote_copy(
                src_ref=src.at[:, columns(to, width)],
                dst_ref=dst.at[u],
                send_sem=send.at[n],
                recv_sem=recv.at[n],
                device_id=(b, to),
                device_id_type=MESH,
            ).start()
        pltpu.make_async_copy(src.at[:, columns(u, width)], dst.at[u], own.at[n]).start()

    def landed(n):
        dst = pairs[n][1]
        wait_bytes(dst.at[pl.ds(0, members - 1)], recv.at[n])
        wait_bytes(dst.at[0], own.at[n])

    spread(0)
    spread(1)
    landed(0)
    landed(1)
    keep_k = pltpu.make_async_copy(land_k, hk, own.at[4])
    keep_v = pltpu.make_async_copy(land_v, hv, own.at[5])
    keep_k.start()
    keep_v.start()
    spread(2)
    spread(3)
    for n, (land, slots, out) in enumerate(((land_k, slots_k, fk), (land_v, slots_v, fv))):
        for t in range(1, groups):
            to = lax.rem(b + t, groups)
            for s in range(NEED):
                slots[t, s] = land[pick[to, s]]
            pltpu.make_async_remote_copy(
                src_ref=slots.at[t],
                dst_ref=out.at[b],
                send_sem=blk_send.at[n],
                recv_sem=blk_recv.at[n],
                device_id=(to, u),
                device_id_type=MESH,
            ).start()
    landed(2)
    landed(3)
    keep_k.wait()
    keep_v.wait()
    for n, out in enumerate((fk, fv)):
        wait_bytes(out.at[pl.ds(0, groups - 1)], blk_recv.at[n])
        wait_bytes(out.at[pl.ds(0, groups - 1)], blk_send.at[n])
    for n in range(4):
        wait_bytes(hq.at[pl.ds(0, members - 1)], send.at[n])


def dot(a, b, contract):
    return lax.dot_general(a, b, ((contract[:1], contract[1:]), ((), ())), preferred_element_type=F32)


def attend_kernel(listed, count, q, k, v, g, fk, fv, o, dq, dk, dv, pk, pv, tiles):
    span = q.shape[0]
    heads = q.shape[2] // HEAD_DIM
    scale = HEAD_DIM ** (-0.5)
    dk[...] = jnp.zeros_like(dk)
    dv[...] = jnp.zeros_like(dv)

    @pl.loop(0, span)
    def _(i):
        start = jnp.clip(i - 1, 0, span - 3)
        n = count[i]
        column = lax.broadcasted_iota(jnp.int32, (BLOCK, 3 * BLOCK), 1) + start * BLOCK
        inside = (column >= (i - 1) * BLOCK) & (column < (i + 2) * BLOCK)
        for h in range(heads):
            hs = slice(h * HEAD_DIM, (h + 1) * HEAD_DIM)
            qi, gi = q[i, :, hs], g[i, :, hs]
            kw = k[pl.ds(start, 3), :, hs].reshape(3 * BLOCK, HEAD_DIM)
            vw = v[pl.ds(start, 3), :, hs].reshape(3 * BLOCK, HEAD_DIM)
            scores = jnp.where(inside, dot(qi, kw, (1, 1)) * scale, -jnp.inf)

            def score(e, peak):
                tile = dot(qi, fk[listed[i, e], :, hs], (1, 1)) * scale
                tiles[h, e] = tile
                return jnp.maximum(peak, jnp.max(tile, axis=1, keepdims=True))

            peak = lax.fori_loop(0, n, score, jnp.max(scores, axis=1, keepdims=True))
            raised = jnp.exp(scores - peak)

            def weigh(e, carry):
                total, out = carry
                tile = jnp.exp(tiles[h, e] - peak)
                tiles[h, e] = tile
                return total + jnp.sum(tile, axis=1, keepdims=True), out

            total, _ = lax.fori_loop(0, n, weigh, (jnp.sum(raised, axis=1, keepdims=True), 0))
            inverse = 1.0 / total
            prob = raised * inverse
            weights = prob.astype(BF16)

            def output(e, out):
                tile = tiles[h, e] * inverse
                tiles[h, e] = tile
                return out + dot(tile.astype(BF16), fv[listed[i, e], :, hs], (1, 0))

            out = lax.fori_loop(0, n, output, dot(weights, vw, (1, 0)))
            o[i, :, hs] = out.astype(BF16)
            delta = jnp.sum(gi.astype(F32) * out, axis=1, keepdims=True)
            dscore = (prob * (dot(gi, vw, (1, 1)) - delta)).astype(BF16)
            dk[pl.ds(start, 3), :, hs] += dot(dscore, qi, (0, 0)).reshape(3, BLOCK, HEAD_DIM)
            dv[pl.ds(start, 3), :, hs] += dot(weights, gi, (0, 0)).reshape(3, BLOCK, HEAD_DIM)

            def grads(e, total):
                slot = listed[i, e]
                tile = tiles[h, e]
                ds = (tile * (dot(gi, fv[slot, :, hs], (1, 1)) - delta)).astype(BF16)
                pk[slot, :, hs] = (dot(ds, qi, (0, 0)) * scale).astype(BF16)
                pv[slot, :, hs] = dot(tile.astype(BF16), gi, (0, 0)).astype(BF16)
                return total + dot(ds, fk[slot, :, hs], (1, 0))

            grad = lax.fori_loop(0, n, grads, dot(dscore, kw, (1, 0)))
            dq[i, :, hs] = (grad * scale).astype(BF16)


def scatter_kernel(
    groups, members, listed, o, dq, dk, dv, pk, pv, out_o, out_q, out_k, out_v,
    back_k, back_v, sum_k, sum_v, send, recv, own, blk_send, blk_recv,
):
    b, u = lax.axis_index("blk"), lax.axis_index("ulysses")
    width = o.shape[2]
    scale = HEAD_DIM ** (-0.5)
    greet(groups, members)
    for n, (part, back) in enumerate(((pk, back_k), (pv, back_v))):
        for t in range(1, groups):
            to = lax.rem(b + t, groups)
            pltpu.make_async_remote_copy(
                src_ref=part.at[to],
                dst_ref=back.at[pl.ds(pl.multiple_of(b * NEED, NEED), NEED)],
                send_sem=blk_send.at[n],
                recv_sem=blk_recv.at[n],
                device_id=(to, u),
                device_id_type=MESH,
            ).start()

    def start_one(n, src, dst, t):
        to = lax.rem(u + t, members)
        pltpu.make_async_remote_copy(
            src_ref=src.at[to],
            dst_ref=dst.at[:, columns(u, width)],
            send_sem=send.at[n],
            recv_sem=recv.at[n],
            device_id=(b, to),
            device_id_type=MESH,
        ).start()

    def start_own(n, src, dst):
        pltpu.make_async_copy(src.at[u], dst.at[:, columns(u, width)], own.at[n]).start()

    for n, (src, dst) in enumerate(((o, out_o), (dq, out_q))):
        for t in range(1, members):
            start_one(n, src, dst, t)
        start_own(n, src, dst)
    for n, (own_part, back, summed, dst, factor) in enumerate(
        ((dk, back_k, sum_k, out_k, scale), (dv, back_v, sum_v, out_v, 1.0))
    ):
        back[groups * NEED] = jnp.zeros(back.shape[1:], BF16)
        wait_bytes(back.at[pl.ds(0, (groups - 1) * NEED)], blk_recv.at[n])
        for t in range(members):
            j = lax.rem(u + 1 + t, members)
            total = own_part[j] * factor
            for e in range(LINKS):
                total = total + back[listed[j, e]].astype(F32)
            summed[j] = total.astype(BF16)
            if t < members - 1:
                start_one(2 + n, summed, dst, t + 1)
        start_own(2 + n, summed, dst)
    for n, dst in enumerate((out_o, out_q, out_k, out_v)):
        wait_bytes(dst.at[:, pl.ds(0, (members - 1) * width)], recv.at[n])
        wait_bytes(dst.at[:, pl.ds(0, (members - 1) * width)], send.at[n])
        wait_bytes(dst.at[:, pl.ds(0, width)], own.at[n])
    for n in range(2):
        wait_bytes(back_k.at[pl.ds(0, (groups - 1) * NEED)], blk_send.at[n])


def tables(block_mask, span, groups, group_id):
    rows = lax.dynamic_slice_in_dim(block_mask, group_id * span, span, 0)
    iota = lambda shape, axis: lax.broadcasted_iota(jnp.int32, shape, axis)
    cube = rows.reshape(span, groups, span) * (iota((span, groups, span), 1) != group_id)
    wanted = jnp.max(cube, axis=0)
    before = (iota((span, span), 0) < iota((span, span), 1)).astype(jnp.int32)
    rank_in = jnp.sum(wanted[:, :, None] * before[None], axis=1)
    has = jnp.sum(cube, axis=2)
    slot_in = jnp.sum(cube * rank_in[None], axis=2)
    before_c = (iota((groups, groups), 0) < iota((groups, groups), 1)).astype(jnp.int32)
    place = jnp.sum(has[:, :, None] * before_c[None], axis=1)
    rank_out = jnp.sum(has[:, None, :] * before[:, :, None], axis=0)
    partner = iota((span, groups), 1)
    spot = iota((span, groups), 0)
    chosen = has[:, :, None] * (place[:, :, None] == iota((span, groups, LINKS), 2))
    list_in = jnp.sum(chosen * (partner * NEED + slot_in)[:, :, None], axis=1)
    list_out = jnp.sum(chosen * (partner * NEED + rank_out)[:, :, None], axis=1)
    count = jnp.sum(has, axis=1)
    list_out = jnp.where(
        iota((span, LINKS), 1) < count[:, None], list_out, groups * NEED
    )
    pick = jnp.sum(
        (has * spot)[:, :, None] * (rank_out[:, :, None] == iota((span, groups, NEED), 2)), axis=0
    )
    return pick, list_in, count, list_out


def shards(query_tokens, key_tokens, value_tokens, cotangent, block_mask):
    groups, members = lax.axis_size("blk"), lax.axis_size("ulysses")
    group_id = lax.axis_index("blk")
    tokens, model = query_tokens.shape
    span = members * tokens // BLOCK
    width = model // members
    pick, list_in, count, list_out = tables(block_mask, span, groups, group_id)
    blocks = jax.ShapeDtypeStruct((span, BLOCK, width), BF16)
    slots = jax.ShapeDtypeStruct((groups, NEED, BLOCK, width), BF16)
    dma = pltpu.SemaphoreType.DMA
    params = functools.partial(pltpu.CompilerParams, vmem_limit_bytes=56 * 2**20)
    hq, hk, hv, hg, fk, fv = pl.pallas_call(
        functools.partial(gather_kernel, groups, members),
        out_shape=(blocks,) * 4 + (slots,) * 2,
        in_specs=[SMEM] + [ANY] * 4,
        out_specs=(ANY,) * 6,
        scratch_shapes=[
            pltpu.VMEM(blocks.shape, BF16),
            pltpu.VMEM(blocks.shape, BF16),
            pltpu.VMEM(slots.shape, BF16),
            pltpu.VMEM(slots.shape, BF16),
            dma((4,)),
            dma((4,)),
            dma((6,)),
            dma((2,)),
            dma((2,)),
        ],
        compiler_params=params(collective_id=0, has_side_effects=True),
        name="gather",
    )(pick, query_tokens, key_tokens, value_tokens, cotangent)
    flat = (groups * NEED, BLOCK, width)
    wide = jax.ShapeDtypeStruct(blocks.shape, F32)
    parts = jax.ShapeDtypeStruct(flat, BF16)
    o, dq, dk, dv, pk, pv = pl.pallas_call(
        attend_kernel,
        out_shape=(blocks, blocks, wide, wide, parts, parts),
        in_specs=[SMEM] * 2 + [VMEM] * 6,
        out_specs=(VMEM,) * 6,
        scratch_shapes=[pltpu.VMEM((width // HEAD_DIM, LINKS, BLOCK, BLOCK), F32)],
        compiler_params=params(),
        name="attend",
    )(list_in, count, hq, hk, hv, hg, fk.reshape(flat), fv.reshape(flat))
    back = pltpu.VMEM((groups * NEED + 1, BLOCK, width), BF16)
    whole = jax.ShapeDtypeStruct((tokens, model), BF16)
    return pl.pallas_call(
        functools.partial(scatter_kernel, groups, members),
        out_shape=(whole,) * 4,
        in_specs=[SMEM] + [ANY] * 2 + [VMEM] * 2 + [ANY] * 2,
        out_specs=(ANY,) * 4,
        scratch_shapes=[
            back,
            back,
            pltpu.VMEM(blocks.shape, BF16),
            pltpu.VMEM(blocks.shape, BF16),
            dma((4,)),
            dma((4,)),
            dma((4,)),
            dma((2,)),
            dma((2,)),
        ],
        compiler_params=params(collective_id=1, has_side_effects=True),
        name="scatter",
    )(list_out, o, dq, dk, dv, pk.reshape(slots.shape), pv.reshape(slots.shape))


def solution(mesh):
    placed = P(("blk", "ulysses"), None)
    return jax.shard_map(
        shards,
        mesh=mesh,
        in_specs=(placed,) * 4 + (P(),),
        out_specs=(placed,) * 4,
        check_vma=False,
    )
```

time: 534 us -> 387 us (0.72)
  the two profiles are of different devices: /device:TPU:56 before, /device:TPU:31 now
where the time goes in v1:
time: 387 us; the launch traced here: 385 us
  Pallas kernels  374 us (97%)
  local copies, waits for them, and re-layouts  7.14 us (2%)
    pallas_call x1, Pallas kernels, shards(): pl.pallas_call(functools.partial(gather_kernel, groups, members), out_sha...  160 us
    pallas_call x1, Pallas kernels, shards(): pl.pallas_call(functools.partial(scatter_kernel, groups, members), out_sh...  152 us
    pallas_call x1, Pallas kernels, shards(): pl.pallas_call(attend_kernel, out_shape=(blocks, blocks, wide, wide, part...  61.1 us

profile of v1, /device:TPU:31, one launch (start us, length us, event | category | flops | bytes accessed | tf_op | source)
XLA Modules:
  0.0 384.8 jit_solution(8782948152020331443)
XLA Ops:
  0.6 0.1 iota.79
  0.7 0.1 iota.80
  0.8 1.4 select_reduce_fusion.2
  2.2 0.1 mul.117
  2.3 0.1 multiply_reduce_fusion.1
  2.4 0.1 reshape.85
  2.5 0.7 multiply_reduce_fusion
  3.2 0.1 multiply_reduce_fusion.3
  3.4 0.7 copy.10.pick
  4.0 160.1 %gather.1 = (bf16[16,128,256]{2,1,0:T(8,128)(2,1)}, bf16[16,128,256]{2,1,0:T(8,128)(2,1)}, bf16[16,128,256]{2,1,0:T(8,128)(2,1)}, bf16[16,128,256]{2,1,0:T(8,128...) custom-call(s32[16,2]{1,0:T(8,128)} %copy.10.pick, bf16[128,4096]{1,0:T(8,128)(2,1)} %q.1, ...), custom_call_target="tpu_custom_call" | custom-call | tf_op jit(solution)/shard_map/gather/pallas_call | solution.py:271
  164.2 0.3 fusion.1
  164.5 0.7 copy.11.listed
  165.2 61.1 %attend.1 = (bf16[16,128,256]{2,1,0:T(8,128)(2,1)}, bf16[16,128,256]{2,1,0:T(8,128)(2,1)}, f32[16,128,256]{2,1,0:T(8,128)}, f32[16,128,256]{2,1,0:T(8,128)}, bf1...) custom-call(s32[16,7]{1,0:T(8,128)} %copy.11.listed, s32[16]{0:T(128)} %get-tuple-element.31.count, ...), custom_call_target="tpu_custom_call" | custom-call | tf_op jit(solution)/shard_map/attend/pallas_call | solution.py:293
  226.3 0.1 copy.9
  226.4 0.0 copy-done.3
  226.4 0.7 fusion.2.listed
  227.1 152.3 %scatter.1 = (bf16[128,4096]{1,0:T(8,128)(2,1)}, bf16[128,4096]{1,0:T(8,128)(2,1)}, bf16[128,4096]{1,0:T(8,128)(2,1)}, bf16[128,4096]{1,0:T(8,128)(2,1)}) custom-call(s32[16,7]{1,0:T(8,128)} %fusion.2.listed, bf16[16,128,256]{2,1,0:T(8,128)(2,1)} %get-tuple-element.22.o, bf16[16,128,256]{2,1,0:T(8,128)(2,1)} %get-tuple-element.23.dq, ...), custom_call_target="tpu_custom_call" | custom-call | tf_op jit(solution)/shard_map/scatter/pallas_call | solution.py:304
  379.4 0.0 copy-start.2
  379.4 0.0 copy-start.1
  379.4 2.4 copy.16
  381.9 0.0 copy-done.2
  381.9 1.0 copy.17
  382.8 1.0 copy.18
  383.8 1.0 copy.19
  (9 shorter events, 0.1 us)
Async XLA Ops:
  165.2 61.2 %copy-start.3 = (s32[16]{0:T(128)S(1)}, s32[16]{0:T(128)}, u32[]{:S(2)}) copy-start(s32[16]{0:T(128)} %get-tuple-element.31.count) | copy-start | bytes 196
  379.4 2.5 copy-start.2
  379.4 3.4 copy-start.1
  381.9 1.9 copy-start

commit v2 on v0

v2 whole, which is shorter than its diff:
```python
import functools
import math

import jax
import jax.numpy as jnp
from jax import lax
from jax.experimental import pallas as pl
from jax.experimental.pallas import tpu as pltpu
from jax.sharding import PartitionSpec as P

HEAD_DIM = 128
BLOCK = 128
NEED = 2
LINKS = 7
EDGES = NEED * LINKS
HEADS_HERE = 2
SCALE = HEAD_DIM ** (-0.5)
SCALE2 = SCALE * math.log2(math.e)
MESH = pl.DeviceIdType.MESH
BF16 = jnp.bfloat16
F32 = jnp.float32
ANY = pl.BlockSpec(memory_space=pl.ANY)
SMEM = pl.BlockSpec(memory_space=pltpu.SMEM)


def dot(a, b, contract):
    return lax.dot_general(a, b, ((contract[:1], contract[1:]), ((), ())), preferred_element_type=F32)


def wait_bytes(ref, sem):
    pltpu.make_async_copy(ref, ref, sem).wait()


def kernel(
    groups, members, offsets, tab, q, k, v, g, out_o, out_q, out_k, out_v,
    land, fetched, slots, back, parts, sends, tiles, peaks, sums, outs, logs, deltas,
    edge_q, edge_k, edge_v, own_q, own_k, own_v,
    in_send, in_recv, in_own, to_send, to_recv, ret_send, ret_recv, end_send, end_recv, end_own,
):
    b, u = lax.axis_index("blk"), lax.axis_index("ulysses")
    span = members
    side = b // (groups // 2)
    shift = members // 4

    def head_columns(member, h):
        owner = lax.rem(member + side * (shift * h), members)
        return pl.ds(pl.multiple_of((owner * HEADS_HERE + h) * HEAD_DIM, HEAD_DIM), HEAD_DIM)

    def across(t, h):
        to = lax.rem(b + t, groups)
        to_side = to // (groups // 2)
        return to, lax.rem(u + members + (side - to_side) * (shift * h), members)

    def entry(name, *index):
        at, shape = offsets[name]
        flat = 0
        for n, i in zip(shape, index):
            flat = flat * n + i
        return tab[at + flat]

    barrier = pltpu.get_barrier_semaphore()
    for t in range(1, members):
        pl.semaphore_signal(
            barrier, inc=1, device_id=(b, lax.rem(u + t, members)), device_id_type=MESH
        )
    for h in range(HEADS_HERE):
        for t in range(1, groups):
            pl.semaphore_signal(barrier, inc=1, device_id=across(t, h), device_id_type=MESH)
    pl.semaphore_wait(barrier, members - 1 + HEADS_HERE * (groups - 1))

    sources = (k, v, q, g)

    def spread(h, n):
        src, dst = sources[n], land[h][n]
        for t in range(1, members):
            to = lax.rem(u + t, members)
            pltpu.make_async_remote_copy(
                src_ref=src.at[:, head_columns(to, h)],
                dst_ref=dst.at[u],
                send_sem=in_send.at[h, n],
                recv_sem=in_recv.at[h, n],
                device_id=(b, to),
                device_id_type=MESH,
            ).start()
        pltpu.make_async_copy(src.at[:, head_columns(u, h)], dst.at[u], in_own.at[h, n]).start()

    def landed(h, n):
        dst = land[h][n]
        wait_bytes(dst.at[pl.ds(0, members - 1)], in_recv.at[h, n])
        wait_bytes(dst.at[0], in_own.at[h, n])

    def send_linked(h):
        for n in range(2):
            src, slot, dst = land[h][n], slots[h][n], fetched[h][n]
            for t in range(1, groups):
                to, there = across(t, h)
                for s in range(NEED):
                    slot[t, s] = src[entry("pick", to, s)]
                pltpu.make_async_remote_copy(
                    src_ref=slot.at[t],
                    dst_ref=dst.at[pl.ds(pl.multiple_of(b * NEED, NEED), NEED)],
                    send_sem=to_send.at[h, n],
                    recv_sem=to_recv.at[h, n],
                    device_id=(to, there),
                    device_id_type=MESH,
                ).start()

    def linked(h):
        for n in range(2):
            wait_bytes(fetched[h][n].at[pl.ds(0, (groups - 1) * NEED)], to_recv.at[h, n])

    def forward(h):
        kr, vr, qr, gr = land[h]
        fk, fv = fetched[h]
        peaks[EDGES] = jnp.full((BLOCK, 1), -1e30, F32)
        sums[EDGES] = jnp.zeros((BLOCK, 1), F32)
        outs[EDGES] = jnp.zeros((BLOCK, HEAD_DIM), F32)

        def cross(c, _):
            made = []
            for s in range(NEED):
                e = c * NEED + s
                slot = entry("slot", e)
                tile = dot(qr[entry("query", e)], fk[slot], (1, 1))
                peak = jnp.max(tile, axis=1, keepdims=True)
                raised = jnp.exp2((tile - peak) * SCALE2)
                total = jnp.sum(raised, axis=1, keepdims=True)
                made.append((e, tile, peak, total, dot(raised.astype(BF16), fv[slot], (1, 0))))
            for e, tile, peak, total, out in made:
                tiles[e], peaks[e], sums[e], outs[e] = tile, peak, total, out
            return 0

        lax.fori_loop(0, LINKS, cross, 0)
        own_k[h][...] = jnp.zeros(own_k[h].shape, F32)
        own_v[h][...] = jnp.zeros(own_v[h].shape, F32)

        def own(half, _):
            made = []
            for r in range(2):
                i = half * 2 + r
                start = jnp.clip(i - 1, 0, span - 3)
                column = lax.broadcasted_iota(jnp.int32, (BLOCK, 3 * BLOCK), 1) + start * BLOCK
                inside = (column >= (i - 1) * BLOCK) & (column < (i + 2) * BLOCK)
                qi, gi = qr[i], gr[i]
                kw = kr[pl.ds(start, 3)].reshape(3 * BLOCK, HEAD_DIM)
                vw = vr[pl.ds(start, 3)].reshape(3 * BLOCK, HEAD_DIM)
                scores = jnp.where(inside, dot(qi, kw, (1, 1)), -1e30)
                edges = [entry("edges", i, e) for e in range(LINKS)]
                peak = jnp.max(scores, axis=1, keepdims=True)
                for e in edges:
                    peak = jnp.maximum(peak, peaks[e])
                raised = jnp.exp2((scores - peak) * SCALE2)
                total = jnp.sum(raised, axis=1, keepdims=True)
                out = dot(raised.astype(BF16), vw, (1, 0))
                for e in edges:
                    factor = jnp.exp2((peaks[e] - peak) * SCALE2)
                    total = total + sums[e] * factor
                    out = out + outs[e] * factor
                inverse = 1.0 / total
                out = out * inverse
                delta = jnp.sum(gi.astype(F32) * out, axis=1, keepdims=True)
                prob = raised * inverse
                dscore = (prob * (dot(gi, vw, (1, 1)) - delta)).astype(BF16)
                made.append((
                    i, start, out.astype(BF16), peak * SCALE2 + jnp.log2(total), delta,
                    dot(dscore, kw, (1, 0)), dot(dscore, qi, (0, 0)), dot(prob.astype(BF16), gi, (0, 0)),
                ))
            for i, start, out, log, delta, grad_q, grad_k, grad_v in made:
                sends[h][0][i], logs[i], deltas[i], own_q[h][i] = out, log, delta, grad_q
                own_k[h][pl.ds(start, 3)] += grad_k.reshape(3, BLOCK, HEAD_DIM)
                own_v[h][pl.ds(start, 3)] += grad_v.reshape(3, BLOCK, HEAD_DIM)
            return 0

        lax.fori_loop(0, span // 2, own, 0)

    def backward(h):
        _, _, qr, gr = land[h]
        fk, fv = fetched[h]
        edge_q[EDGES] = jnp.zeros((BLOCK, HEAD_DIM), F32)

        def cross(c, _):
            made = []
            for s in range(NEED):
                e = c * NEED + s
                slot, i = entry("slot", e), entry("query", e)
                qi, gi = qr[i], gr[i]
                prob = jnp.exp2(tiles[e] * SCALE2 - logs[i])
                dscore = (prob * (dot(gi, fv[slot], (1, 1)) - deltas[i])).astype(BF16)
                made.append((
                    e, dot(dscore, fk[slot], (1, 0)), (dot(dscore, qi, (0, 0)) * SCALE).astype(BF16),
                    dot(prob.astype(BF16), gi, (0, 0)).astype(BF16),
                ))
            for e, grad_q, grad_k, grad_v in made:
                edge_q[e], edge_k[e], edge_v[e] = grad_q, grad_k, grad_v
            return 0

        lax.fori_loop(0, LINKS, cross, 0)

    def send_back(h):
        for n, made in enumerate((edge_k, edge_v)):
            part, dst = parts[h][n], back[h][n]
            for t in range(1, groups):
                to, there = across(t, h)
                for s in range(NEED):
                    part[t, s] = made[entry("edge", to, s)]
                pltpu.make_async_remote_copy(
                    src_ref=part.at[t],
                    dst_ref=dst.at[pl.ds(pl.multiple_of(b * NEED, NEED), NEED)],
                    send_sem=ret_send.at[h, n],
                    recv_sem=ret_recv.at[h, n],
                    device_id=(to, there),
                    device_id_type=MESH,
                ).start()

    results = (out_o, out_q, out_k, out_v)

    def finish(h, n):
        src, dst = sends[h][n], results[n].at[:, head_columns(u, h)]
        for t in range(1, members):
            to = lax.rem(u + t, members)
            pltpu.make_async_remote_copy(
                src_ref=src.at[to],
                dst_ref=dst,
                send_sem=end_send.at[h, n],
                recv_sem=end_recv.at[h, n],
                device_id=(b, to),
                device_id_type=MESH,
            ).start()
        pltpu.make_async_copy(src.at[u], dst, end_own.at[h, n]).start()

    def queries(h):
        def one(i, _):
            total = own_q[h][i]
            for e in range(LINKS):
                total = total + edge_q[entry("edges", i, e)]
            sends[h][1][i] = (total * SCALE).astype(BF16)
            return 0

        lax.fori_loop(0, span, one, 0)

    def keys(h):
        for n, (own_part, factor) in enumerate(((own_k[h], SCALE), (own_v[h], 1.0))):
            got = back[h][n]
            got[groups * NEED] = jnp.zeros((BLOCK, HEAD_DIM), BF16)
            wait_bytes(got.at[pl.ds(0, (groups - 1) * NEED)], ret_recv.at[h, n])

            def one(j, _):
                total = own_part[j] * factor
                for e in range(LINKS):
                    total = total + got[entry("back", j, e)].astype(F32)
                sends[h][2 + n][j] = total.astype(BF16)
                return 0

            lax.fori_loop(0, span, one, 0)
            finish(h, 2 + n)

    spread(0, 0)
    spread(0, 1)
    landed(0, 0)
    landed(0, 1)
    spread(0, 2)
    spread(0, 3)
    send_linked(0)
    landed(0, 2)
    landed(0, 3)
    spread(1, 0)
    spread(1, 1)
    linked(0)
    forward(0)
    finish(0, 0)
    landed(1, 0)
    landed(1, 1)
    spread(1, 2)
    spread(1, 3)
    send_linked(1)
    backward(0)
    send_back(0)
    queries(0)
    finish(0, 1)
    landed(1, 2)
    landed(1, 3)
    linked(1)
    forward(1)
    finish(1, 0)
    backward(1)
    send_back(1)
    keys(0)
    queries(1)
    finish(1, 1)
    keys(1)
    for h in range(HEADS_HERE):
        for n in range(2):
            wait_bytes(fetched[h][n].at[pl.ds(0, (groups - 1) * NEED)], to_send.at[h, n])
            wait_bytes(back[h][n].at[pl.ds(0, (groups - 1) * NEED)], ret_send.at[h, n])
        for n in range(4):
            most = land[h][n].at[pl.ds(0, members - 1)]
            wait_bytes(most, in_send.at[h, n])
            wait_bytes(most, end_send.at[h, n])
            wait_bytes(most, end_recv.at[h, n])
            wait_bytes(land[h][n].at[0], end_own.at[h, n])


def tables(block_mask, span, groups, group_id):
    rows = lax.dynamic_slice_in_dim(block_mask, group_id * span, span, 0)
    iota = lambda shape, axis: lax.broadcasted_iota(jnp.int32, shape, axis)
    cube = rows.reshape(span, groups, span) * (iota((span, groups, span), 1) != group_id)
    wanted = jnp.max(cube, axis=0)
    linked = jnp.max(wanted, axis=1)
    before = (iota((span, span), 0) < iota((span, span), 1)).astype(jnp.int32)
    before_c = (iota((groups, groups), 0) < iota((groups, groups), 1)).astype(jnp.int32)
    rank_in = jnp.sum(wanted[:, :, None] * before[None], axis=1)
    link = jnp.sum(linked[:, None] * before_c, axis=0)
    has = jnp.sum(cube, axis=2)
    slot_in = jnp.sum(cube * rank_in[None], axis=2)
    place = jnp.sum(has[:, :, None] * before_c[None], axis=1)
    rank_out = jnp.sum(has[:, None, :] * before[:, :, None], axis=0)
    partner = iota((span, groups), 1)
    spot = iota((span, groups), 0)
    chosen = has[:, :, None] * (place[:, :, None] == iota((span, groups, LINKS), 2))
    edges = jnp.sum(chosen * (link[None] * NEED + slot_in)[:, :, None], axis=1)
    returns = jnp.sum(chosen * (partner * NEED + rank_out)[:, :, None], axis=1)
    valid = iota((span, LINKS), 1) < jnp.sum(has, axis=1)[:, None]
    pick = jnp.sum(
        (has * spot)[:, :, None] * (rank_out[:, :, None] == iota((span, groups, NEED), 2)), axis=0
    )
    link_is = linked[:, None] * (link[:, None] == iota((groups, EDGES), 1) // NEED)
    slot = jnp.sum(link_is * (iota((groups, EDGES), 0) * NEED + iota((groups, EDGES), 1) % NEED), axis=0)
    number = link[None] * NEED + slot_in
    query = jnp.sum(
        (has * spot)[:, :, None] * (number[:, :, None] == iota((span, groups, EDGES), 2)), axis=(0, 1)
    )
    edge = jnp.minimum(link[:, None] * NEED + iota((groups, NEED), 1), EDGES - 1)
    named = {
        "pick": pick,
        "edge": edge,
        "slot": slot,
        "query": query,
        "edges": jnp.where(valid, edges, EDGES),
        "back": jnp.where(valid, returns, groups * NEED),
    }
    offsets, at = {}, 0
    for name, array in named.items():
        offsets[name] = (at, array.shape)
        at += array.size
    return jnp.concatenate([array.reshape(-1) for array in named.values()]), offsets


def shards(query_tokens, key_tokens, value_tokens, cotangent, block_mask):
    groups, members = lax.axis_size("blk"), lax.axis_size("ulysses")
    tokens, model = query_tokens.shape
    span = members * tokens // BLOCK
    table, offsets = tables(block_mask, span, groups, lax.axis_index("blk"))
    dma = pltpu.SemaphoreType.DMA
    blocks = lambda n, dtype: pltpu.VMEM((n, BLOCK, HEAD_DIM), dtype)
    column = lambda n: pltpu.VMEM((n, BLOCK, 1), F32)
    pairs = lambda: pltpu.VMEM((groups, NEED, BLOCK, HEAD_DIM), BF16)
    each = lambda n, make: [[make() for _ in range(n)] for _ in range(HEADS_HERE)]
    whole = jax.ShapeDtypeStruct((tokens, model), BF16)
    return pl.pallas_call(
        functools.partial(kernel, groups, members, offsets),
        out_shape=(whole,) * 4,
        in_specs=[SMEM] + [ANY] * 4,
        out_specs=(ANY,) * 4,
        scratch_shapes=[
            each(4, lambda: blocks(span, BF16)),
            each(2, lambda: blocks(groups * NEED, BF16)),
            each(2, pairs),
            each(2, lambda: blocks(groups * NEED + 1, BF16)),
            each(2, pairs),
            each(4, lambda: blocks(span, BF16)),
            blocks(EDGES, F32),
            column(EDGES + 1),
            column(EDGES + 1),
            blocks(EDGES + 1, F32),
            column(span),
            column(span),
            blocks(EDGES + 1, F32),
            blocks(EDGES, BF16),
            blocks(EDGES, BF16),
            [blocks(span, F32) for _ in range(HEADS_HERE)],
            [blocks(span, F32) for _ in range(HEADS_HERE)],
            [blocks(span, F32) for _ in range(HEADS_HERE)],
        ]
        + [dma((HEADS_HERE, n)) for n in (4, 4, 4, 2, 2, 2, 2, 4, 4, 4)],
        compiler_params=pltpu.CompilerParams(
            collective_id=0, has_side_effects=True, vmem_limit_bytes=56 * 2**20
        ),
        name="attention",
    )(table, query_tokens, key_tokens, value_tokens, cotangent)


def solution(mesh):
    placed = P(("blk", "ulysses"), None)
    return jax.shard_map(
        shards,
        mesh=mesh,
        in_specs=(placed,) * 4 + (P(),),
        out_specs=(placed,) * 4,
        check_vma=False,
    )
```

time: 534 us -> 298 us (0.56)
  the two profiles are of different devices: /device:TPU:56 before, /device:TPU:31 now
where the time goes in v2:
time: 298 us
  Pallas kernels  286 us (96%)
  local copies, waits for them, and re-layouts  8.17 us (3%)
    pallas_call x1, Pallas kernels, shards(): pl.pallas_call(functools.partial(kernel, groups, members, offsets), out_s...  286 us
    unnamed x10, local copies, waits for them, and re-layouts  6.55 us

profile of v2, /device:TPU:31, one launch (start us, length us, event | category | flops | bytes accessed | tf_op | source)
XLA Modules:
  0.0 298.0 jit_solution(17926297917442819526)
XLA Ops:
  0.8 0.1 iota.127
  0.9 0.8 select_reduce_fusion.3
  1.8 0.1 reduce_max.22
  1.9 0.1 multiply_reduce_fusion.2
  2.0 0.1 select_reduce_fusion.5
  2.1 0.1 multiply_reduce_fusion.4
  2.3 0.1 min.12
  2.4 0.1 reshape.110
  2.5 0.7 multiply_reduce_fusion.1
  3.2 0.3 select_reduce_fusion.1
  3.5 0.1 multiply_reduce_fusion
  3.7 0.1 copy.9
  3.8 0.1 reshape.111
  3.9 0.3 fusion.1
  4.3 0.1 select_n.36
  4.5 0.1 select_n.34
  4.6 0.7 concatenate.3.tab
  5.2 286.2 %attention.1 = (bf16[128,4096]{1,0:T(8,128)(2,1)}, bf16[128,4096]{1,0:T(8,128)(2,1)}, bf16[128,4096]{1,0:T(8,128)(2,1)}, bf16[128,4096]{1,0:T(8,128)(2,1)}) custom-call(s32[316]{0:T(512)} %concatenate.3.tab, bf16[128,4096]{1,0:T(8,128)(2,1)} %q.1, bf16[128,4096]{1,0:T(8,128)(2,1)} %k.1, bf16[128,4096]{1,0:T(8,128)(2,1)} %v.1, bf16[128,4096]{1,0:T(8,128)(2,1)} %g.1), custom_call_target="tpu_custom_call" | custom-call | tf_op jit(solution)/shard_map/attention/pallas_call | solution.py:359
  291.4 2.4 copy.16
  293.8 1.0 copy.17
  294.8 0.6 copy-done.1
  295.4 1.0 copy.18
  296.4 0.6 copy-done
  297.0 1.0 copy.19
  (20 shorter events, 0.5 us)
Async XLA Ops:
  291.4 2.4 copy-start.2
  293.8 1.6 copy-start.1
  295.4 1.6 copy-start

commit v3 on v2

--- a/solution.py
+++ b/solution.py
@@ -32,24 +32,32 @@
 
 
 def kernel(
-    groups, members, offsets, tab, q, k, v, g, out_o, out_q, out_k, out_v,
-    land, fetched, slots, back, parts, sends, tiles, peaks, sums, outs, logs, deltas,
-    edge_q, edge_k, edge_v, own_q, own_k, own_v,
-    in_send, in_recv, in_own, to_send, to_recv, ret_send, ret_recv, end_send, end_recv, end_own,
+    groups, members, cap, offsets, tab, q, k, v, g, out_o, out_q, out_k, out_v,
+    land, fetched, slots, relayed, crossing, crossed, back, parts, relay_parts, relay_back, returning,
+    sends, tiles, peaks, sums, outs, logs, deltas, edge_q, edge_k, edge_v, own_q, own_k, own_v,
+    in_send, in_recv, in_own, to_send, to_recv, over_send, over_recv, ret_send, ret_recv,
+    mid_send, mid_recv, home_send, home_recv, end_send, end_recv, end_own,
 ):
     b, u = lax.axis_index("blk"), lax.axis_index("ulysses")
     span = members
-    side = b // (groups // 2)
+    near = groups // 2
+    side = b // near
     shift = members // 4
+    mirror = lax.rem(b + near, groups)
+    spot = lax.rem(b, near)
 
     def head_columns(member, h):
         owner = lax.rem(member + side * (shift * h), members)
         return pl.ds(pl.multiple_of((owner * HEADS_HERE + h) * HEAD_DIM, HEAD_DIM), HEAD_DIM)
 
-    def across(t, h):
-        to = lax.rem(b + t, groups)
-        to_side = to // (groups // 2)
-        return to, lax.rem(u + members + (side - to_side) * (shift * h), members)
+    def opposite(h):
+        return mirror, lax.rem(u + members + (2 * side - 1) * (shift * h), members)
+
+    def neighbour(t):
+        return lax.rem(spot + t, near)
+
+    def pair(n):
+        return pl.ds(pl.multiple_of(n * NEED, NEED), NEED)
 
     def entry(name, *index):
         at, shape = offsets[name]
@@ -63,10 +71,13 @@
         pl.semaphore_signal(
             barrier, inc=1, device_id=(b, lax.rem(u + t, members)), device_id_type=MESH
         )
+    for t in range(1, near):
+        pl.semaphore_signal(
+            barrier, inc=1, device_id=(side * near + neighbour(t), u), device_id_type=MESH
+        )
     for h in range(HEADS_HERE):
-        for t in range(1, groups):
-            pl.semaphore_signal(barrier, inc=1, device_id=across(t, h), device_id_type=MESH)
-    pl.semaphore_wait(barrier, members - 1 + HEADS_HERE * (groups - 1))
+        pl.semaphore_signal(barrier, inc=1, device_id=opposite(h), device_id_type=MESH)
+    pl.semaphore_wait(barrier, members - 1 + near - 1 + HEADS_HERE)
 
     sources = (k, v, q, g)
 
@@ -89,25 +100,42 @@
         wait_bytes(dst.at[pl.ds(0, members - 1)], in_recv.at[h, n])
         wait_bytes(dst.at[0], in_own.at[h, n])
 
+    def send(src, dst, to, send_sem, recv_sem):
+        pltpu.make_async_remote_copy(
+            src_ref=src, dst_ref=dst, send_sem=send_sem, recv_sem=recv_sem,
+            device_id=to, device_id_type=MESH,
+        ).start()
+
+    def send_crossing(h):
+        for n in range(2):
+            for c in range(cap):
+                crossing[h][n][c] = land[h][n][entry("cross", c)]
+                send(crossing[h][n].at[c], crossed[h][n].at[c], opposite(h), over_send.at[h, n], over_recv.at[h, n])
+
     def send_linked(h):
         for n in range(2):
-            src, slot, dst = land[h][n], slots[h][n], fetched[h][n]
-            for t in range(1, groups):
-                to, there = across(t, h)
+            slot = slots[h][n]
+            for t in range(1, near):
+                to = side * near + neighbour(t)
                 for s in range(NEED):
-                    slot[t, s] = src[entry("pick", to, s)]
-                pltpu.make_async_remote_copy(
-                    src_ref=slot.at[t],
-                    dst_ref=dst.at[pl.ds(pl.multiple_of(b * NEED, NEED), NEED)],
-                    send_sem=to_send.at[h, n],
-                    recv_sem=to_recv.at[h, n],
-                    device_id=(to, there),
-                    device_id_type=MESH,
-                ).start()
+                    slot[t, s] = land[h][n][entry("pick", to, s)]
+                send(slot.at[t], fetched[h][n].at[pair(b)], (to, u), to_send.at[h, n], to_recv.at[h, n])
+
+    def relay(h):
+        for n in range(2):
+            got, slot = crossed[h][n], relayed[h][n]
+            wait_bytes(got, over_recv.at[h, n])
+            for s in range(NEED):
+                fetched[h][n][mirror * NEED + s] = got[entry("relay", spot, s)]
+            for t in range(1, near):
+                for s in range(NEED):
+                    slot[t, s] = got[entry("relay", neighbour(t), s)]
+                to = side * near + neighbour(t)
+                send(slot.at[t], fetched[h][n].at[pair(mirror)], (to, u), to_send.at[h, n], to_recv.at[h, n])
 
     def linked(h):
         for n in range(2):
-            wait_bytes(fetched[h][n].at[pl.ds(0, (groups - 1) * NEED)], to_recv.at[h, n])
+            wait_bytes(fetched[h][n].at[pl.ds(0, 2 * (near - 1) * NEED)], to_recv.at[h, n])
 
     def forward(h):
         kr, vr, qr, gr = land[h]
@@ -198,19 +226,28 @@
 
     def send_back(h):
         for n, made in enumerate((edge_k, edge_v)):
-            part, dst = parts[h][n], back[h][n]
-            for t in range(1, groups):
-                to, there = across(t, h)
+            part, relay_part = parts[h][n], relay_parts[h][n]
+            for s in range(NEED):
+                relay_back[h][n][spot * NEED + s] = made[entry("edge", mirror, s)]
+            for t in range(1, near):
+                to = neighbour(t)
                 for s in range(NEED):
-                    part[t, s] = made[entry("edge", to, s)]
-                pltpu.make_async_remote_copy(
-                    src_ref=part.at[t],
-                    dst_ref=dst.at[pl.ds(pl.multiple_of(b * NEED, NEED), NEED)],
-                    send_sem=ret_send.at[h, n],
-                    recv_sem=ret_recv.at[h, n],
-                    device_id=(to, there),
-                    device_id_type=MESH,
-                ).start()
+                    relay_part[t, s] = made[entry("edge", lax.rem(side + 1, 2) * near + to, s)]
+                    part[t, s] = made[entry("edge", side * near + to, s)]
+                there = (side * near + to, u)
+                send(relay_part.at[t], relay_back[h][n].at[pair(spot)], there, mid_send.at[h, n], mid_recv.at[h, n])
+                send(part.at[t], back[h][n].at[pair(spot)], there, ret_send.at[h, n], ret_recv.at[h, n])
+
+    def relay_home(h):
+        for n in range(2):
+            got = relay_back[h][n]
+            wait_bytes(got.at[pl.ds(0, (near - 1) * NEED)], mid_recv.at[h, n])
+            for c in range(cap):
+                returning[h][n][c] = got[entry("return", c)]
+                send(
+                    returning[h][n].at[c], back[h][n].at[near * NEED + c], opposite(h),
+                    home_send.at[h, n], home_recv.at[h, n],
+                )
 
     results = (out_o, out_q, out_k, out_v)
 
@@ -241,8 +278,9 @@
     def keys(h):
         for n, (own_part, factor) in enumerate(((own_k[h], SCALE), (own_v[h], 1.0))):
             got = back[h][n]
-            got[groups * NEED] = jnp.zeros((BLOCK, HEAD_DIM), BF16)
-            wait_bytes(got.at[pl.ds(0, (groups - 1) * NEED)], ret_recv.at[h, n])
+            got[near * NEED + cap] = jnp.zeros((BLOCK, HEAD_DIM), BF16)
+            wait_bytes(got.at[pl.ds(0, (near - 1) * NEED)], ret_recv.at[h, n])
+            wait_bytes(got.at[pl.ds(0, cap)], home_recv.at[h, n])
 
             def one(j, _):
                 total = own_part[j] * factor
@@ -256,23 +294,27 @@
 
     spread(0, 0)
     spread(0, 1)
+    spread(1, 0)
+    spread(1, 1)
     landed(0, 0)
     landed(0, 1)
+    send_crossing(0)
+    landed(1, 0)
+    landed(1, 1)
+    send_crossing(1)
     spread(0, 2)
     spread(0, 3)
     send_linked(0)
+    send_linked(1)
+    spread(1, 2)
+    spread(1, 3)
+    relay(0)
+    relay(1)
     landed(0, 2)
     landed(0, 3)
-    spread(1, 0)
-    spread(1, 1)
     linked(0)
     forward(0)
     finish(0, 0)
-    landed(1, 0)
-    landed(1, 1)
-    spread(1, 2)
-    spread(1, 3)
-    send_linked(1)
     backward(0)
     send_back(0)
     queries(0)
@@ -284,14 +326,20 @@
     finish(1, 0)
     backward(1)
     send_back(1)
-    keys(0)
+    relay_home(0)
     queries(1)
     finish(1, 1)
+    relay_home(1)
+    keys(0)
     keys(1)
     for h in range(HEADS_HERE):
         for n in range(2):
-            wait_bytes(fetched[h][n].at[pl.ds(0, (groups - 1) * NEED)], to_send.at[h, n])
-            wait_bytes(back[h][n].at[pl.ds(0, (groups - 1) * NEED)], ret_send.at[h, n])
+            most = fetched[h][n].at[pl.ds(0, (near - 1) * NEED)]
+            wait_bytes(fetched[h][n].at[pl.ds(0, 2 * (near - 1) * NEED)], to_send.at[h, n])
+            wait_bytes(most, mid_send.at[h, n])
+            wait_bytes(most, ret_send.at[h, n])
+            wait_bytes(crossing[h][n], over_send.at[h, n])
+            wait_bytes(returning[h][n], home_send.at[h, n])
         for n in range(4):
             most = land[h][n].at[pl.ds(0, members - 1)]
             wait_bytes(most, in_send.at[h, n])
@@ -300,8 +348,12 @@
             wait_bytes(land[h][n].at[0], end_own.at[h, n])
 
 
-def tables(block_mask, span, groups, group_id):
+def tables(block_mask, span, groups, group_id, cap):
+    near = groups // 2
     rows = lax.dynamic_slice_in_dim(block_mask, group_id * span, span, 0)
+    mirror = (group_id + near) % groups
+    other_rows = lax.dynamic_slice_in_dim(block_mask, mirror * span, span, 0)
+    far_from = lambda who: (iota((1, groups), 1) // near != who // near).astype(jnp.int32)
     iota = lambda shape, axis: lax.broadcasted_iota(jnp.int32, shape, axis)
     cube = rows.reshape(span, groups, span) * (iota((span, groups, span), 1) != group_id)
     wanted = jnp.max(cube, axis=0)
@@ -318,7 +370,24 @@
     spot = iota((span, groups), 0)
     chosen = has[:, :, None] * (place[:, :, None] == iota((span, groups, LINKS), 2))
     edges = jnp.sum(chosen * (link[None] * NEED + slot_in)[:, :, None], axis=1)
-    returns = jnp.sum(chosen * (partner * NEED + rank_out)[:, :, None], axis=1)
+    far = far_from(group_id)
+    far_has = has * far
+    far_place = jnp.sum(jnp.sum(far_has, axis=0)[:, None] * before_c, axis=0)[None] + rank_out
+    from_back = jnp.where(far > 0, near * NEED + far_place, partner % near * NEED + rank_out)
+    returns = jnp.sum(chosen * from_back[:, :, None], axis=1)
+    cross = jnp.sum(
+        (far_has * spot)[:, :, None] * (far_place[:, :, None] == iota((span, groups, cap), 2)), axis=(0, 1)
+    )
+    other = jnp.sum(other_rows.reshape(span, groups, span), axis=(0, 2))[:, None] * far_from(mirror).reshape(groups, 1)
+    other_place = jnp.sum(other * before_c, axis=0)[:, None] + iota((groups, NEED), 1)
+    other_used = (iota((groups, NEED), 1) < other).astype(jnp.int32)
+    toward = iota((groups, NEED), 0) % near
+    relay = lax.dynamic_slice_in_dim(jnp.minimum(other_place, cap - 1), group_id // near * near, near, 0)
+    give_back = jnp.sum(
+        (other_used * (toward * NEED + iota((groups, NEED), 1)))[:, :, None]
+        * (other_place[:, :, None] == iota((groups, NEED, cap), 2)),
+        axis=(0, 1),
+    )
     valid = iota((span, LINKS), 1) < jnp.sum(has, axis=1)[:, None]
     pick = jnp.sum(
         (has * spot)[:, :, None] * (rank_out[:, :, None] == iota((span, groups, NEED), 2)), axis=0
@@ -332,11 +401,14 @@
     edge = jnp.minimum(link[:, None] * NEED + iota((groups, NEED), 1), EDGES - 1)
     named = {
         "pick": pick,
+        "cross": cross,
+        "relay": relay,
+        "return": give_back,
         "edge": edge,
         "slot": slot,
         "query": query,
         "edges": jnp.where(valid, edges, EDGES),
-        "back": jnp.where(valid, returns, groups * NEED),
+        "back": jnp.where(valid, returns, near * NEED + cap),
     }
     offsets, at = {}, 0
     for name, array in named.items():
@@ -349,15 +421,17 @@
     groups, members = lax.axis_size("blk"), lax.axis_size("ulysses")
     tokens, model = query_tokens.shape
     span = members * tokens // BLOCK
-    table, offsets = tables(block_mask, span, groups, lax.axis_index("blk"))
+    cap = EDGES
+    near = groups // 2
+    table, offsets = tables(block_mask, span, groups, lax.axis_index("blk"), cap)
     dma = pltpu.SemaphoreType.DMA
     blocks = lambda n, dtype: pltpu.VMEM((n, BLOCK, HEAD_DIM), dtype)
     column = lambda n: pltpu.VMEM((n, BLOCK, 1), F32)
-    pairs = lambda: pltpu.VMEM((groups, NEED, BLOCK, HEAD_DIM), BF16)
+    pairs = lambda: pltpu.VMEM((near, NEED, BLOCK, HEAD_DIM), BF16)
     each = lambda n, make: [[make() for _ in range(n)] for _ in range(HEADS_HERE)]
     whole = jax.ShapeDtypeStruct((tokens, model), BF16)
     return pl.pallas_call(
-        functools.partial(kernel, groups, members, offsets),
+        functools.partial(kernel, groups, members, cap, offsets),
         out_shape=(whole,) * 4,
         in_specs=[SMEM] + [ANY] * 4,
         out_specs=(ANY,) * 4,
@@ -365,8 +439,14 @@
             each(4, lambda: blocks(span, BF16)),
             each(2, lambda: blocks(groups * NEED, BF16)),
             each(2, pairs),
-            each(2, lambda: blocks(groups * NEED + 1, BF16)),
             each(2, pairs),
+            each(2, lambda: blocks(cap, BF16)),
+            each(2, lambda: blocks(cap, BF16)),
+            each(2, lambda: blocks(near * NEED + cap + 1, BF16)),
+            each(2, pairs),
+            each(2, pairs),
+            each(2, lambda: blocks(near * NEED, BF16)),
+            each(2, lambda: blocks(cap, BF16)),
             each(4, lambda: blocks(span, BF16)),
             blocks(EDGES, F32),
             column(EDGES + 1),
@@ -381,7 +461,7 @@
             [blocks(span, F32) for _ in range(HEADS_HERE)],
             [blocks(span, F32) for _ in range(HEADS_HERE)],
         ]
-        + [dma((HEADS_HERE, n)) for n in (4, 4, 4, 2, 2, 2, 2, 4, 4, 4)],
+        + [dma((HEADS_HERE, n)) for n in (4, 4, 4, 2, 2, 2, 2, 2, 2, 2, 2, 2, 2, 4, 4, 4)],
         compiler_params=pltpu.CompilerParams(
             collective_id=0, has_side_effects=True, vmem_limit_bytes=56 * 2**20
         ),

time: 298 us -> 269 us (0.903); the launches traced: 298 us -> 266 us
  Pallas kernels: 286 us -> 253 us
    pallas_call x1, Pallas kernels: 286 us -> 253 us  [shards(): pl.pallas_call(functools.partial(kernel, groups, members, cap, offsets),...]
where the time goes in v3:
time: 269 us; the launch traced here: 266 us
  Pallas kernels  253 us (94%)
  local copies, waits for them, and re-layouts  8.41 us (3%)
  other arithmetic  4.03 us (1%)
    pallas_call x1, Pallas kernels, shards(): pl.pallas_call(functools.partial(kernel, groups, members, cap, offsets),...  253 us
    unnamed x10, local copies, waits for them, and re-layouts  6.55 us

profile of v3, /device:TPU:31, one launch (start us, length us, event | category | flops | bytes accessed | tf_op | source)
XLA Modules:
  0.0 265.9 jit_solution(15211662105988134020)
XLA Ops:
  0.9 0.1 iota.201
  1.0 0.9 select_reduce_fusion.4
  1.9 0.1 reduce_max.22
  2.0 0.1 multiply_reduce_fusion.2
  2.2 0.1 multiply_reduce_fusion.4
  2.6 0.1 reduce_sum.177
  3.1 0.4 fusion.2
  3.4 0.1 reshape.348
  3.5 0.7 multiply_reduce_fusion.1
  4.2 0.1 multiply_reduce_fusion
  4.4 0.1 select_reduce_fusion.8
  4.5 0.3 select_reduce_fusion.1
  4.8 0.3 select_reduce_fusion.2
  5.2 0.3 fusion.1
  5.8 0.1 reshape.349
  6.0 0.1 select_n.111
  6.1 0.7 concatenate.3.tab
  6.7 252.6 %attention.1 = (bf16[128,4096]{1,0:T(8,128)(2,1)}, bf16[128,4096]{1,0:T(8,128)(2,1)}, bf16[128,4096]{1,0:T(8,128)(2,1)}, bf16[128,4096]{1,0:T(8,128)(2,1)}) custom-call(s32[360]{0:T(512)} %concatenate.3.tab, bf16[128,4096]{1,0:T(8,128)(2,1)} %q.1, bf16[128,4096]{1,0:T(8,128)(2,1)} %k.1, bf16[128,4096]{1,0:T(8,128)(2,1)} %v.1, bf16[128,4096]{1,0:T(8,128)(2,1)} %g.1), custom_call_target="tpu_custom_call" | custom-call | tf_op jit(solution)/shard_map/attention/pallas_call | solution.py:433
  259.4 2.4 copy.17
  261.7 1.0 copy.18
  262.7 0.6 copy-done.1
  263.3 1.0 copy.19
  264.3 0.6 copy-done
  264.9 1.0 copy.20
  (36 shorter events, 1.3 us)
Async XLA Ops:
  259.4 2.4 copy-start.2
  261.7 1.6 copy-start.1
  263.3 1.6 copy-start

commit v4 on v3

--- a/solution.py
+++ b/solution.py
@@ -13,6 +13,7 @@
 NEED = 2
 LINKS = 7
 EDGES = NEED * LINKS
+FEW = 8
 HEADS_HERE = 2
 SCALE = HEAD_DIM ** (-0.5)
 SCALE2 = SCALE * math.log2(math.e)
@@ -126,10 +127,10 @@
             got, slot = crossed[h][n], relayed[h][n]
             wait_bytes(got, over_recv.at[h, n])
             for s in range(NEED):
-                fetched[h][n][mirror * NEED + s] = got[entry("relay", spot, s)]
+                fetched[h][n][mirror * NEED + s] = got[jnp.minimum(entry("relay", spot, s), cap - 1)]
             for t in range(1, near):
                 for s in range(NEED):
-                    slot[t, s] = got[entry("relay", neighbour(t), s)]
+                    slot[t, s] = got[jnp.minimum(entry("relay", neighbour(t), s), cap - 1)]
                 to = side * near + neighbour(t)
                 send(slot.at[t], fetched[h][n].at[pair(mirror)], (to, u), to_send.at[h, n], to_recv.at[h, n])
 
@@ -278,7 +279,7 @@
     def keys(h):
         for n, (own_part, factor) in enumerate(((own_k[h], SCALE), (own_v[h], 1.0))):
             got = back[h][n]
-            got[near * NEED + cap] = jnp.zeros((BLOCK, HEAD_DIM), BF16)
+            got[near * NEED + EDGES] = jnp.zeros((BLOCK, HEAD_DIM), BF16)
             wait_bytes(got.at[pl.ds(0, (near - 1) * NEED)], ret_recv.at[h, n])
             wait_bytes(got.at[pl.ds(0, cap)], home_recv.at[h, n])
 
@@ -348,7 +349,7 @@
             wait_bytes(land[h][n].at[0], end_own.at[h, n])
 
 
-def tables(block_mask, span, groups, group_id, cap):
+def tables(block_mask, span, groups, group_id):
     near = groups // 2
     rows = lax.dynamic_slice_in_dim(block_mask, group_id * span, span, 0)
     mirror = (group_id + near) % groups
@@ -376,16 +377,16 @@
     from_back = jnp.where(far > 0, near * NEED + far_place, partner % near * NEED + rank_out)
     returns = jnp.sum(chosen * from_back[:, :, None], axis=1)
     cross = jnp.sum(
-        (far_has * spot)[:, :, None] * (far_place[:, :, None] == iota((span, groups, cap), 2)), axis=(0, 1)
+        (far_has * spot)[:, :, None] * (far_place[:, :, None] == iota((span, groups, EDGES), 2)), axis=(0, 1)
     )
     other = jnp.sum(other_rows.reshape(span, groups, span), axis=(0, 2))[:, None] * far_from(mirror).reshape(groups, 1)
     other_place = jnp.sum(other * before_c, axis=0)[:, None] + iota((groups, NEED), 1)
     other_used = (iota((groups, NEED), 1) < other).astype(jnp.int32)
     toward = iota((groups, NEED), 0) % near
-    relay = lax.dynamic_slice_in_dim(jnp.minimum(other_place, cap - 1), group_id // near * near, near, 0)
+    relay = lax.dynamic_slice_in_dim(other_place, group_id // near * near, near, 0)
     give_back = jnp.sum(
         (other_used * (toward * NEED + iota((groups, NEED), 1)))[:, :, None]
-        * (other_place[:, :, None] == iota((groups, NEED, cap), 2)),
+        * (other_place[:, :, None] == iota((groups, NEED, EDGES), 2)),
         axis=(0, 1),
     )
     valid = iota((span, LINKS), 1) < jnp.sum(has, axis=1)[:, None]
@@ -408,7 +409,7 @@
         "slot": slot,
         "query": query,
         "edges": jnp.where(valid, edges, EDGES),
-        "back": jnp.where(valid, returns, near * NEED + cap),
+        "back": jnp.where(valid, returns, near * NEED + EDGES),
     }
     offsets, at = {}, 0
     for name, array in named.items():
@@ -417,20 +418,28 @@
     return jnp.concatenate([array.reshape(-1) for array in named.values()]), offsets
 
 
+def most_crossing(block_mask, span, groups):
+    blocks = block_mask.shape[0]
+    iota = lambda shape, axis: lax.broadcasted_iota(jnp.int32, shape, axis)
+    side = lambda axis: iota(block_mask.shape, axis) // (blocks // 2)
+    rows = jnp.sum(jnp.where(side(0) != side(1), block_mask, 0), axis=1, keepdims=True)
+    belongs = iota((blocks, groups), 0) // span == iota((blocks, groups), 1)
+    return jnp.max(jnp.sum(jnp.where(belongs, rows, 0), axis=0))
+
+
 def shards(query_tokens, key_tokens, value_tokens, cotangent, block_mask):
     groups, members = lax.axis_size("blk"), lax.axis_size("ulysses")
     tokens, model = query_tokens.shape
     span = members * tokens // BLOCK
-    cap = EDGES
     near = groups // 2
-    table, offsets = tables(block_mask, span, groups, lax.axis_index("blk"), cap)
+    table, offsets = tables(block_mask, span, groups, lax.axis_index("blk"))
     dma = pltpu.SemaphoreType.DMA
     blocks = lambda n, dtype: pltpu.VMEM((n, BLOCK, HEAD_DIM), dtype)
     column = lambda n: pltpu.VMEM((n, BLOCK, 1), F32)
     pairs = lambda: pltpu.VMEM((near, NEED, BLOCK, HEAD_DIM), BF16)
     each = lambda n, make: [[make() for _ in range(n)] for _ in range(HEADS_HERE)]
     whole = jax.ShapeDtypeStruct((tokens, model), BF16)
-    return pl.pallas_call(
+    call = lambda cap, name, collective_id: pl.pallas_call(
         functools.partial(kernel, groups, members, cap, offsets),
         out_shape=(whole,) * 4,
         in_specs=[SMEM] + [ANY] * 4,
@@ -442,7 +451,7 @@
             each(2, pairs),
             each(2, lambda: blocks(cap, BF16)),
             each(2, lambda: blocks(cap, BF16)),
-            each(2, lambda: blocks(near * NEED + cap + 1, BF16)),
+            each(2, lambda: blocks(near * NEED + EDGES + 1, BF16)),
             each(2, pairs),
             each(2, pairs),
             each(2, lambda: blocks(near * NEED, BF16)),
@@ -463,10 +472,16 @@
         ]
         + [dma((HEADS_HERE, n)) for n in (4, 4, 4, 2, 2, 2, 2, 2, 2, 2, 2, 2, 2, 4, 4, 4)],
         compiler_params=pltpu.CompilerParams(
-            collective_id=0, has_side_effects=True, vmem_limit_bytes=56 * 2**20
+            collective_id=collective_id, has_side_effects=True, vmem_limit_bytes=56 * 2**20
         ),
-        name="attention",
-    )(table, query_tokens, key_tokens, value_tokens, cotangent)
+        name=name,
+    )
+    return lax.cond(
+        most_crossing(block_mask, span, groups) <= FEW,
+        call(FEW, "attention_few", 0),
+        call(EDGES, "attention_most", 1),
+        table, query_tokens, key_tokens, value_tokens, cotangent,
+    )
 
 
 def solution(mesh):

time: 269 us -> 255 us (0.948)
  Pallas kernels: 253 us -> 236 us
    pallas_call x1, Pallas kernels: 253 us -> 236 us  [shards(): lax.cond(most_crossing(block_mask, span, groups) <= FEW, call(FEW, 'atten...]
where the time goes in v4:
time: 255 us; the launch traced here: 251 us
  Pallas kernels  236 us (93%)
  local copies, waits for them, and re-layouts  6.43 us (3%)
  other arithmetic  6.01 us (2%)
    pallas_call x1, Pallas kernels, shards(): lax.cond(most_crossing(block_mask, span, groups) <= FEW, call(FEW, 'atten...  236 us
    unnamed x10, local copies, waits for them, and re-layouts  5.15 us

profile of v4, /device:TPU:31, one launch (start us, length us, event | category | flops | bytes accessed | tf_op | source)
XLA Modules:
  0.0 250.8 jit_solution(13527370064617221528)
XLA Ops:
  0.9 0.1 iota.248
  1.0 1.2 select_reduce_fusion
  2.2 0.1 select_reduce_fusion.5
  2.3 0.6 reduce_max.29
  3.6 0.9 select_reduce_fusion.6
  4.6 0.1 reduce_max.32
  4.7 0.1 multiply_reduce_fusion.2
  4.9 0.1 multiply_reduce_fusion.4
  5.2 0.1 reduce_sum.197
  5.7 0.4 fusion.2
  6.1 0.1 reshape.349
  6.2 0.7 multiply_reduce_fusion.1
  6.9 0.1 multiply_reduce_fusion
  7.1 0.3 select_reduce_fusion.2
  7.5 0.3 select_reduce_fusion.3
  7.8 0.3 fusion.1
  8.8 236.8 %conditional.1 = ((bf16[128,4096]{1,0:T(8,128)(2,1)S(1)}, bf16[128,4096]{1,0:T(8,128)(2,1)S(1)}, bf16[128,4096]{1,0:T(8,128)(2,1)}, bf16[128,4096]{1,0:T(8,128)(2,1)})) conditional(s32[]{:T(128)} %convert_element_type.43, (s32[360]{0:T(512)S(1)}, bf16[128,4096]{1,0:T(8,128)(2,1)S(1)}, bf16[128,4096]{1,0:T(8,128)(2,1)}, ...), branch_computations={%region_24.25_spmd, %region_25.26_spmd} | conditional | bytes 8 | solution.py:479
  9.2 236.4 %attention_few.1 = (bf16[128,4096]{1,0:T(8,128)(2,1)S(1)}, bf16[128,4096]{1,0:T(8,128)(2,1)S(1)}, bf16[128,4096]{1,0:T(8,128)(2,1)}, bf16[128,4096]{1,0:T(8,128)(2,1)}) custom-call(s32[360]{0:T(512)S(1)} %get-tuple-element.25.tab, bf16[128,4096]{1,0:T(8,128)(2,1)S(1)} %get-tuple-element.55.q, bf16[128,4096]{1,0:T(8,128)(2,1)} %get-tuple-element.57.k, ...), custom_call_target="tpu_custom_call" | custom-call | tf_op jit(solution)/shard_map/cond/branch_1_fun/attention_few/pallas_call | solution.py:479
  245.7 1.0 copy.41
  246.6 1.0 copy.42
  247.6 0.6 copy-done.1
  248.2 1.0 copy.43
  249.2 0.6 copy-done.2
  249.8 1.0 copy.44
  (43 shorter events, 1.6 us)
Async XLA Ops:
  0.6 8.2 %copy-start = (bf16[128,4096]{1,0:T(8,128)(2,1)S(1)}, bf16[128,4096]{1,0:T(8,128)(2,1)}, u32[]{:S(2)}) copy-start(bf16[128,4096]{1,0:T(8,128)(2,1)} %param.7) | copy-start | bytes 3145732
  246.6 1.6 copy-start.1
  248.2 1.6 copy-start.2

commit v5 on v4

--- a/solution.py
+++ b/solution.py
@@ -35,7 +35,7 @@
 def kernel(
     groups, members, cap, offsets, tab, q, k, v, g, out_o, out_q, out_k, out_v,
     land, fetched, slots, relayed, crossing, crossed, back, parts, relay_parts, relay_back, returning,
-    sends, tiles, peaks, sums, outs, logs, deltas, edge_q, edge_k, edge_v, own_q, own_k, own_v,
+    sends, tiles, peaks, sums, outs, logs, deltas, edge_q, edge_k, edge_v, own_k, own_v, probs,
     in_send, in_recv, in_own, to_send, to_recv, over_send, over_recv, ret_send, ret_recv,
     mid_send, mid_recv, home_send, home_recv, end_send, end_recv, end_own,
 ):
@@ -160,8 +160,6 @@
             return 0
 
         lax.fori_loop(0, LINKS, cross, 0)
-        own_k[h][...] = jnp.zeros(own_k[h].shape, F32)
-        own_v[h][...] = jnp.zeros(own_v[h].shape, F32)
 
         def own(half, _):
             made = []
@@ -188,14 +186,37 @@
                 inverse = 1.0 / total
                 out = out * inverse
                 delta = jnp.sum(gi.astype(F32) * out, axis=1, keepdims=True)
-                prob = raised * inverse
-                dscore = (prob * (dot(gi, vw, (1, 1)) - delta)).astype(BF16)
+                made.append((i, out.astype(BF16), peak * SCALE2 + jnp.log2(total), delta, raised * inverse))
+            for i, out, log, delta, prob in made:
+                sends[h][0][i], logs[h][i], deltas[h][i], probs[h][i] = out, log, delta, prob
+            return 0
+
+        lax.fori_loop(0, span // 2, own, 0)
+
+    def own_backward(h):
+        kr, vr, qr, gr = land[h]
+        own_k[h][...] = jnp.zeros(own_k[h].shape, F32)
+        own_v[h][...] = jnp.zeros(own_v[h].shape, F32)
+
+        def own(half, _):
+            made = []
+            for r in range(2):
+                i = half * 2 + r
+                start = jnp.clip(i - 1, 0, span - 3)
+                qi, gi = qr[i], gr[i]
+                kw = kr[pl.ds(start, 3)].reshape(3 * BLOCK, HEAD_DIM)
+                vw = vr[pl.ds(start, 3)].reshape(3 * BLOCK, HEAD_DIM)
+                prob = probs[h][i]
+                dscore = (prob * (dot(gi, vw, (1, 1)) - deltas[h][i])).astype(BF16)
+                grad_q = dot(dscore, kw, (1, 0))
+                for e in range(LINKS):
+                    grad_q = grad_q + edge_q[h][entry("edges", i, e)]
                 made.append((
-                    i, start, out.astype(BF16), peak * SCALE2 + jnp.log2(total), delta,
-                    dot(dscore, kw, (1, 0)), dot(dscore, qi, (0, 0)), dot(prob.astype(BF16), gi, (0, 0)),
+                    i, start, (grad_q * SCALE).astype(BF16),
+                    dot(dscore, qi, (0, 0)), dot(prob.astype(BF16), gi, (0, 0)),
                 ))
-            for i, start, out, log, delta, grad_q, grad_k, grad_v in made:
-                sends[h][0][i], logs[i], deltas[i], own_q[h][i] = out, log, delta, grad_q
+            for i, start, grad_q, grad_k, grad_v in made:
+                sends[h][1][i] = grad_q
                 own_k[h][pl.ds(start, 3)] += grad_k.reshape(3, BLOCK, HEAD_DIM)
                 own_v[h][pl.ds(start, 3)] += grad_v.reshape(3, BLOCK, HEAD_DIM)
             return 0
@@ -205,7 +226,7 @@
     def backward(h):
         _, _, qr, gr = land[h]
         fk, fv = fetched[h]
-        edge_q[EDGES] = jnp.zeros((BLOCK, HEAD_DIM), F32)
+        edge_q[h][EDGES] = jnp.zeros((BLOCK, HEAD_DIM), F32)
 
         def cross(c, _):
             made = []
@@ -213,14 +234,14 @@
                 e = c * NEED + s
                 slot, i = entry("slot", e), entry("query", e)
                 qi, gi = qr[i], gr[i]
-                prob = jnp.exp2(tiles[e] * SCALE2 - logs[i])
-                dscore = (prob * (dot(gi, fv[slot], (1, 1)) - deltas[i])).astype(BF16)
+                prob = jnp.exp2(tiles[e] * SCALE2 - logs[h][i])
+                dscore = (prob * (dot(gi, fv[slot], (1, 1)) - deltas[h][i])).astype(BF16)
                 made.append((
                     e, dot(dscore, fk[slot], (1, 0)), (dot(dscore, qi, (0, 0)) * SCALE).astype(BF16),
                     dot(prob.astype(BF16), gi, (0, 0)).astype(BF16),
                 ))
             for e, grad_q, grad_k, grad_v in made:
-                edge_q[e], edge_k[e], edge_v[e] = grad_q, grad_k, grad_v
+                edge_q[h][e], edge_k[e], edge_v[e] = grad_q, grad_k, grad_v
             return 0
 
         lax.fori_loop(0, LINKS, cross, 0)
@@ -265,16 +286,6 @@
                 device_id_type=MESH,
             ).start()
         pltpu.make_async_copy(src.at[u], dst, end_own.at[h, n]).start()
-
-    def queries(h):
-        def one(i, _):
-            total = own_q[h][i]
-            for e in range(LINKS):
-                total = total + edge_q[entry("edges", i, e)]
-            sends[h][1][i] = (total * SCALE).astype(BF16)
-            return 0
-
-        lax.fori_loop(0, span, one, 0)
 
     def keys(h):
         for n, (own_part, factor) in enumerate(((own_k[h], SCALE), (own_v[h], 1.0))):
@@ -318,7 +329,7 @@
     finish(0, 0)
     backward(0)
     send_back(0)
-    queries(0)
+    own_backward(0)
     finish(0, 1)
     landed(1, 2)
     landed(1, 3)
@@ -328,10 +339,10 @@
     backward(1)
     send_back(1)
     relay_home(0)
-    queries(1)
-    finish(1, 1)
     relay_home(1)
     keys(0)
+    own_backward(1)
+    finish(1, 1)
     keys(1)
     for h in range(HEADS_HERE):
         for n in range(2):
@@ -461,14 +472,14 @@
             column(EDGES + 1),
             column(EDGES + 1),
             blocks(EDGES + 1, F32),
-            column(span),
-            column(span),
-            blocks(EDGES + 1, F32),
+            [column(span) for _ in range(HEADS_HERE)],
+            [column(span) for _ in range(HEADS_HERE)],
+            [blocks(EDGES + 1, F32) for _ in range(HEADS_HERE)],
             blocks(EDGES, BF16),
             blocks(EDGES, BF16),
             [blocks(span, F32) for _ in range(HEADS_HERE)],
             [blocks(span, F32) for _ in range(HEADS_HERE)],
-            [blocks(span, F32) for _ in range(HEADS_HERE)],
+            [pltpu.VMEM((span, BLOCK, 3 * BLOCK), F32) for _ in range(HEADS_HERE)],
         ]
         + [dma((HEADS_HERE, n)) for n in (4, 4, 4, 2, 2, 2, 2, 2, 2, 2, 2, 2, 2, 4, 4, 4)],
         compiler_params=pltpu.CompilerParams(

time: 255 us -> 254 us (level)
  no operation moved by 1% of the time
where the time goes in v5:
time: 254 us; the launch traced here: 250 us
  Pallas kernels  236 us (93%)
  local copies, waits for them, and re-layouts  6.43 us (3%)
  other arithmetic  6.01 us (2%)
    pallas_call x1, Pallas kernels, shards(): lax.cond(most_crossing(block_mask, span, groups) <= FEW, call(FEW, 'atten...  236 us
    unnamed x10, local copies, waits for them, and re-layouts  5.15 us

profile of v5, /device:TPU:31, one launch (start us, length us, event | category | flops | bytes accessed | tf_op | source)
XLA Modules:
  0.0 250.2 jit_solution(7186602489801315871)
XLA Ops:
  0.9 0.1 iota.248
  1.0 1.2 select_reduce_fusion
  2.2 0.1 select_reduce_fusion.5
  2.3 0.6 reduce_max.29
  3.6 0.9 select_reduce_fusion.6
  4.6 0.1 reduce_max.32
  4.7 0.1 multiply_reduce_fusion.2
  4.9 0.1 multiply_reduce_fusion.4
  5.2 0.1 reduce_sum.197
  5.7 0.4 fusion.2
  6.1 0.1 reshape.349
  6.2 0.7 multiply_reduce_fusion.1
  6.9 0.1 multiply_reduce_fusion
  7.1 0.3 select_reduce_fusion.2
  7.5 0.3 select_reduce_fusion.3
  7.8 0.3 fusion.1
  8.8 236.3 %conditional.1 = ((bf16[128,4096]{1,0:T(8,128)(2,1)S(1)}, bf16[128,4096]{1,0:T(8,128)(2,1)S(1)}, bf16[128,4096]{1,0:T(8,128)(2,1)}, bf16[128,4096]{1,0:T(8,128)(2,1)})) conditional(s32[]{:T(128)} %convert_element_type.43, (s32[360]{0:T(512)S(1)}, bf16[128,4096]{1,0:T(8,128)(2,1)S(1)}, bf16[128,4096]{1,0:T(8,128)(2,1)}, ...), branch_computations={%region_24.25_spmd, %region_25.26_spmd} | conditional | bytes 8 | solution.py:490
  9.2 235.9 %attention_few.1 = (bf16[128,4096]{1,0:T(8,128)(2,1)S(1)}, bf16[128,4096]{1,0:T(8,128)(2,1)S(1)}, bf16[128,4096]{1,0:T(8,128)(2,1)}, bf16[128,4096]{1,0:T(8,128)(2,1)}) custom-call(s32[360]{0:T(512)S(1)} %get-tuple-element.25.tab, bf16[128,4096]{1,0:T(8,128)(2,1)S(1)} %get-tuple-element.55.q, bf16[128,4096]{1,0:T(8,128)(2,1)} %get-tuple-element.57.k, ...), custom_call_target="tpu_custom_call" | custom-call | tf_op jit(solution)/shard_map/cond/branch_1_fun/attention_few/pallas_call | solution.py:490
  245.1 1.0 copy.41
  246.1 1.0 copy.42
  247.0 0.6 copy-done.1
  247.7 1.0 copy.43
  248.6 0.6 copy-done.2
  249.3 1.0 copy.44
  (43 shorter events, 1.6 us)
Async XLA Ops:
  0.6 8.2 %copy-start = (bf16[128,4096]{1,0:T(8,128)(2,1)S(1)}, bf16[128,4096]{1,0:T(8,128)(2,1)}, u32[]{:S(2)}) copy-start(bf16[128,4096]{1,0:T(8,128)(2,1)} %param.7) | copy-start | bytes 3145732
  246.1 1.6 copy-start.1
  247.7 1.6 copy-start.2
